TPU v7x, 32 devices: a whole 2x2x4 slice. The times are simulated.
32 devices in a mesh: dp: 4 (over z), node: 4 (over x, core), local: 2 (over y).
Axes of the slice: x: 2, y: 2, z: 4, core: 2. Of those that a mesh axis runs over, the one named last changes fastest.
Arguments:
- d_out: bfloat16 [2048, 7168], P(('dp', 'node'), 'local'), may hold values from -6 to 6
- logits: float32 [2048, 4], P(('dp', 'node')), may hold values from -6 to 6
- groups: int32 [2048, 2], P(('dp', 'node')), may hold values from 0 to 3, as said below
- slots: int32 [2048, 2], P(('dp', 'node')), may hold values from -1 to 71, as said below
- hidden_act: bfloat16 [4, 4, 4, 72, 1024], P('dp', 'node'), may hold values from -6 to 6
- w_down: bfloat16 [4, 1024, 7168], P('node', None, 'local'), may hold values from -0.1875 to 0.1875
Outputs:
- d_logits: float32 [2048, 4], P(('dp', 'node'))
- d_hidden: bfloat16 [4, 4, 4, 72, 1024], P('dp', 'node', None, None, 'local')
- d_wdown: bfloat16 [4, 1024, 7168], P('node', 'dp', 'local')
Inputs may be any that keep to these rules, and one draw needn't show every extreme that they name: `groups`: each row names 2 different experts. `slots`: a live route's slot is its rank among the routes to that expert of the 128 rows of its source device, counted in order of token and then of position in the row; routes whose rank reaches 72 are dropped and hold -1.
All inputs are finite; a program needn't handle non-finite values.
Results may differ from a plain program's by a relative error of at most 0.009.
Values may be sent and summed in bfloat16 or wider, within the bound.
A program may use at most 64 MiB of HBM per device.

v0:
```python
import jax
import jax.numpy as jnp
from jax import lax
from jax.sharding import PartitionSpec as P

route_scale = 2.5


def shards(d_out, logits, groups, slots, hidden_act, w_down):
    node_count = lax.axis_size("node")
    expert_count = logits.shape[1]
    cap_rows = hidden_act.shape[3]
    hid_units = hidden_act.shape[4]
    feat_local = d_out.shape[1]
    scores = jax.nn.sigmoid(logits)
    picked = (groups[..., None] == jnp.arange(expert_count, dtype=jnp.int32)).astype(jnp.float32)
    chosen = jnp.sum(picked * scores[:, None, :], axis=-1)
    totals = jnp.sum(chosen, axis=-1, keepdims=True)
    gates = (route_scale * chosen / totals).astype(jnp.bfloat16)
    target = jnp.where(slots >= 0, groups * cap_rows + slots, -1)
    placed = (target[..., None] == jnp.arange(expert_count * cap_rows, dtype=jnp.int32)).astype(
        jnp.float32
    )
    send_rows = jnp.einsum(
        "tkc,td->cd", placed.astype(jnp.bfloat16), d_out, preferred_element_type=jnp.float32
    )
    send_rows = send_rows.astype(jnp.bfloat16).reshape(expert_count, cap_rows, feat_local)
    send_gates = jnp.einsum(
        "tkc,tk->c", placed, gates.astype(jnp.float32), precision=lax.Precision.HIGHEST
    )
    send_gates = send_gates.astype(jnp.bfloat16).reshape(expert_count, cap_rows)
    recv_rows, recv_gates = (
        lax.all_to_all(send_rows, "node", split_axis=0, concat_axis=0, tiled=True),
        lax.all_to_all(send_gates, "node", split_axis=0, concat_axis=0, tiled=True),
    )
    rows = recv_rows.reshape(node_count * cap_rows, feat_local)
    row_gate = recv_gates.reshape(node_count * cap_rows).astype(jnp.float32)
    act_rows = hidden_act.reshape(node_count * cap_rows, hid_units)
    weight = w_down.reshape(hid_units, feat_local)
    expert_out = jnp.dot(act_rows, weight, preferred_element_type=jnp.float32)
    dot_part = jnp.sum(rows.astype(jnp.float32) * expert_out, axis=-1)
    term = lax.dot_general(
        weight, rows, (((1,), (1,)), ((), ())), preferred_element_type=jnp.float32
    )
    summed = lax.psum_scatter(
        (term * row_gate[None, :]).astype(jnp.bfloat16), "local", scatter_dimension=0, tiled=True
    ).astype(jnp.float32)
    d_hidden = summed.T.astype(jnp.bfloat16).reshape(1, 1, node_count, cap_rows, summed.shape[0])
    scaled = (row_gate[:, None] * rows.astype(jnp.float32)).astype(jnp.bfloat16)
    weight_term = lax.dot_general(
        act_rows, scaled, (((0,), (0,)), ((), ())), preferred_element_type=jnp.float32
    )
    weight_sum = lax.psum_scatter(
        weight_term.astype(jnp.bfloat16), "dp", scatter_dimension=0, tiled=True
    ).astype(jnp.float32)
    d_wdown = weight_sum.astype(jnp.bfloat16).reshape(1, weight_sum.shape[0], feat_local)
    outgoing = lax.psum(dot_part, "local")
    returned = lax.all_to_all(
        outgoing.reshape(node_count, cap_rows), "node", split_axis=0, concat_axis=0, tiled=True
    ).reshape(node_count * cap_rows)
    route_dot = jnp.einsum("tkc,c->tk", placed, returned, precision=lax.Precision.HIGHEST)
    shares = chosen / totals
    mean_dot = jnp.sum(shares * route_dot, axis=-1, keepdims=True)
    d_chosen = route_scale * (route_dot - mean_dot) / totals
    d_logits = jnp.einsum("tke,tk->te", picked, d_chosen * chosen * (1.0 - chosen))
    return (d_logits, d_hidden, d_wdown)


def solution(mesh):
    in_specs = (
        P(("dp", "node"), "local"),
        P(("dp", "node"), None),
        P(("dp", "node"), None),
        P(("dp", "node"), None),
        P("dp", "node", None, None, None),
        P("node", None, "local"),
    )
    out_specs = (
        P(("dp", "node"), None),
        P("dp", "node", None, None, "local"),
        P("node", "dp", "local"),
    )
    return jax.shard_map(shards, mesh=mesh, in_specs=in_specs, out_specs=out_specs, check_vma=False)
```

profile of v0, /device:TPU:0, one launch (start us, length us, event | category | flops | bytes accessed | tf_op | source)
XLA Modules:
  0.0 227.9 jit_solution(2984479064483478207)
XLA Ops:
  7.2 0.0 copy-start
  7.2 0.8 compare_select_fusion
  8.0 0.4 copy-done
  8.4 2.0 fusion.30
  10.4 0.0 copy-start.2
  10.4 4.3 %all-to-all-start = ((bf16[4,72,3584]{2,1,0:T(8,128)(2,1)}), bf16[4,72,3584]{2,1,0:T(8,128)(2,1)S(1)}, u32[]{:S(2)}, u32[]{:S(2)}) async-start(bf16[4,72,3584]{2,1,0:T(8,128)(2,1)} %bitcast), calls=%async_computation | async-start | bytes 4128768 | tf_op jit(solution)/shard_map/all_to_all | solution.py:33
  14.7 0.0 copy-done.2
  14.7 25.3 %all-to-all-done = bf16[4,72,3584]{2,1,0:T(8,128)(2,1)S(1)} async-done(((bf16[4,72,3584]{2,1,0:T(8,128)(2,1)}), bf16[4,72,3584]{2,1,0:T(8,128)(2,1)S(1)}, u32[]{:S(2)}, u32[]{:S(2)}) %all-to-all-start) | async-done | bytes 2064416 | tf_op jit(solution)/shard_map/all_to_all | solution.py:33
  40.1 0.0 copy-start.1
  40.1 5.8 %fusion.8 = f32[288]{0:T(512)S(1)} fusion(bf16[288,1024]{1,0:T(8,128)(2,1)} %bitcast.47, bf16[1,1024,3584]{2,1,0:T(8,128)(2,1)} %param.11, bf16[288,3584]{1,0:T(8,128)(2,1)S(1)} %bitcast.40), kind=kOutput, calls=%fused_computation.9 | convolution fusion | flops 2117025536 | bytes 9995392 | tf_op jit(solution)/shard_map/dot_general | solution.py:40
  45.9 0.1 all_to_all.16
  45.9 5.8 %psum.7 = f32[4,1,72]{2,1,0:T(1,128)} all-reduce(f32[4,1,72]{2,1,0:T(1,128)S(1)} %all_to_all.16), channel_id=1, replica_groups=mesh['dp'=4,'node'=4,'local'=2] {'local'}, use_global_device_ids=true, to_apply=%region_2.3 | all-reduce | flops 288 | bytes 2304 | tf_op jit(solution)/shard_map/psum | solution.py:57
  51.7 3.2 %all-to-all-start.1 = ((f32[4,1,72]{2,1,0:T(1,128)}), f32[4,1,72]{2,1,0:T(1,128)S(1)}, u32[]{:S(2)}, u32[]{:S(2)}) async-start(f32[4,1,72]{2,1,0:T(1,128)} %psum.7), calls=%async_computation.1 | async-start | bytes 4096 | tf_op jit(solution)/shard_map/all_to_all | solution.py:58
  55.0 0.0 reduce-scatter.5.cloned.1.call-start
  55.0 0.0 copy-done.1
  55.0 3.6 %all-to-all-done.1 = f32[4,1,72]{2,1,0:T(1,128)S(1)} async-done(((f32[4,1,72]{2,1,0:T(1,128)}), f32[4,1,72]{2,1,0:T(1,128)S(1)}, u32[]{:S(2)}, u32[]{:S(2)}) %all-to-all-start.1) | async-done | bytes 1184 | tf_op jit(solution)/shard_map/all_to_all | solution.py:58
  58.6 0.5 broadcast.37
  59.1 0.7 reduce.12
  59.8 0.1 reshape.73
  59.9 0.2 fusion.21
  60.1 0.2 convolution_reduce_fusion
  60.3 0.1 all_to_all.20
  60.4 6.1 %all_to_all.24 = bf16[4,1,72]{2,1,0:T(2,128)(2,1)S(1)} all-to-all(bf16[4,1,72]{2,1,0:T(2,128)(2,1)S(1)} %all_to_all.20), channel_id=1, replica_groups=mesh['dp'=4,'node'=4,'local'=2] {'node'}, dimensions={0} | all-to-all | bytes 1152 | tf_op jit(solution)/shard_map/all_to_all | solution.py:34
  66.5 0.0 copy-start.3
  66.5 0.5 multiply_convert_fusion
  67.0 0.5 copy-done.3
  67.5 6.1 %fusion.4 = bf16[1024,3584]{0,1:T(8,128)(2,1)} fusion(bf16[288,3584]{1,0:T(8,128)(2,1)S(1)} %bitcast.42, bf16[288,1024]{1,0:T(8,128)(2,1)S(1)} %bitcast.48), kind=kOutput, calls=%fused_computation.5 | convolution fusion | flops 2117599232 | bytes 9994240 | tf_op jit(solution)/shard_map/dot_general | solution.py:50
  73.6 0.0 reduce-scatter.5.cloned.1.call-update
  73.6 0.0 reduce-scatter.3.cloned.1.call-start
  73.7 0.1 reshape.71
  73.8 6.2 %fusion.17 = bf16[1024,288]{0,1:T(8,128)(2,1)} fusion(bf16[288,3584]{1,0:T(8,128)(2,1)S(1)} %bitcast.41, bf16[1,1024,3584]{2,1,0:T(8,128)(2,1)} %param.11, f32[288]{0:T(512)S(1)} %reshape.71), kind=kOutput, calls=%fused_computation.12 | convolution fusion | flops 2114519040 | bytes 9995392 | tf_op jit(solution)/shard_map/dot_general | solution.py:42
  80.0 0.0 reduce-scatter.3.cloned.1.call-update
  80.1 0.6 select_reduce_fusion.2
  80.7 121.7 %reduce-scatter.5.cloned.1.call-done = bf16[256,3584]{0,1:T(8,128)(2,1)} async-done(((bf16[1024,3584]{0,1:T(8,128)(2,1)}), bf16[256,3584]{0,1:T(8,128)(2,1)}) %reduce-scatter.5.cloned.1.call-update) | async-done | bytes 1835024 | tf_op jit(solution)/shard_map/reduce_scatter | solution.py:53
  202.4 3.8 %copy.23 = bf16[1,256,3584]{2,1,0:T(8,128)(2,1)} copy(bf16[1,256,3584]{1,2,0:T(8,128)(2,1)} %bitcast.43) | data formatting | bytes 3670016
  206.2 14.8 %reduce-scatter.3.cloned.1.call-done = bf16[512,288]{0,1:T(8,128)(2,1)} async-done(((bf16[1024,288]{0,1:T(8,128)(2,1)}), bf16[512,288]{0,1:T(8,128)(2,1)}) %reduce-scatter.3.cloned.1.call-update) | async-done | bytes 294928 | tf_op jit(solution)/shard_map/reduce_scatter | solution.py:45
  (7 shorter events, 0.1 us)
Async XLA Ops:
  7.2 1.2 copy-start
  10.4 4.3 %copy-start.2 = (f32[128,4]{0,1:T(4,128)S(1)}, f32[128,4]{0,1:T(4,128)}, u32[]{:S(2)}) copy-start(f32[128,4]{0,1:T(4,128)} %param.7) | copy-start | bytes 6148
  10.4 29.7 %all-to-all-start = ((bf16[4,72,3584]{2,1,0:T(8,128)(2,1)}), bf16[4,72,3584]{2,1,0:T(8,128)(2,1)S(1)}, u32[]{:S(2)}, u32[]{:S(2)}) async-start(bf16[4,72,3584]{2,1,0:T(8,128)(2,1)} %bitcast), calls=%async_computation | async-start | bytes 4128768 | tf_op jit(solution)/shard_map/all_to_all | solution.py:33
  40.1 14.9 %copy-start.1 = (s32[128,2]{0,1:T(2,128)S(1)}, s32[128,2]{0,1:T(2,128)}, u32[]{:S(2)}) copy-start(s32[128,2]{0,1:T(2,128)} %param.8) | copy-start | bytes 3076
  51.7 6.9 %all-to-all-start.1 = ((f32[4,1,72]{2,1,0:T(1,128)}), f32[4,1,72]{2,1,0:T(1,128)S(1)}, u32[]{:S(2)}, u32[]{:S(2)}) async-start(f32[4,1,72]{2,1,0:T(1,128)} %psum.7), calls=%async_computation.1 | async-start | bytes 4096 | tf_op jit(solution)/shard_map/all_to_all | solution.py:58
  55.0 147.4 %reduce-scatter.5.cloned.1.call-start = ((), (), s32[]{:S(2)}) async-start(), calls=%async_computation.6 | async-start | bytes 9175040 | tf_op jit(solution)/shard_map/reduce_scatter | solution.py:53
  66.5 1.1 copy-start.3
  73.6 147.4 %reduce-scatter.3.cloned.1.call-start = ((), (), s32[]{:S(2)}) async-start(), calls=%async_computation.5 | async-start | bytes 884736 | tf_op jit(solution)/shard_map/reduce_scatter | solution.py:45
Sparse Core Ops, SparseCore 0:
  73.8 128.5 reduce-scatter.4
  205.2 15.7 reduce-scatter.2
where the time goes:
time: 228 us
  waiting for transfers between devices  166 us (73%)
  matrix products  20.5 us (9%)
  between operations  14.1 us (6%)
  blocking collectives  11.9 us (5%)
  starting transfers between devices  7.64 us (3%)
  local copies, waits for them, and re-layouts  5.57 us (2%)
  other arithmetic  2.71 us (1%)
    reduce_scatter x1, waiting for transfers between devices, shards(): lax.psum_scatter(weight_term.astype(jnp.bfloat16), 'dp', scatter_dimensio...  122 us
    all_to_all x1, waiting for transfers between devices, shards(): lax.all_to_all(send_rows, 'node', split_axis=0, concat_axis=0, tiled=True)  25.3 us
    reduce_scatter x1, waiting for transfers between devices, shards(): lax.psum_scatter((term * row_gate[None, :]).astype(jnp.bfloat16), 'local'...  14.8 us
    dot_general x1, matrix products, shards(): lax.dot_general(weight, rows, (((1,), (1,)), ((), ())), preferred_element...  6.25 us
    all_to_all x1, blocking collectives, shards(): lax.all_to_all(send_gates, 'node', split_axis=0, concat_axis=0, tiled=True)  6.08 us
    dot_general x1, matrix products, shards(): lax.dot_general(act_rows, scaled, (((0,), (0,)), ((), ())), preferred_ele...  6.08 us
    psum x1, blocking collectives, shards(): outgoing = lax.psum(dot_part, 'local')  5.79 us
    dot_general x1, matrix products, shards(): expert_out = jnp.dot(act_rows, weight, preferred_element_type=jnp.float32)  5.77 us
  transfers between devices with their start and end apart: 4, of which 4 were waited for; matrix products, arithmetic and copies ran while one was open for 5% of the time, Pallas kernels for 0%

commit v1 on v0

--- a/solution.py
+++ b/solution.py
@@ -1,9 +1,304 @@
+import functools
+
 import jax
 import jax.numpy as jnp
 from jax import lax
+from jax.experimental import pallas as pl
+from jax.experimental.pallas import tpu as pltpu
 from jax.sharding import PartitionSpec as P
 
 route_scale = 2.5
+gather_limit = 20 * 1024 * 1024
+chunk_rows = 32
+
+
+def peer(**where):
+    return dict(device_id=where, device_id_type=pl.DeviceIdType.MESH)
+
+
+def greet(peers):
+    barrier = pltpu.get_barrier_semaphore()
+    for where in peers:
+        pl.semaphore_signal(barrier, inc=1, **where)
+    pl.semaphore_wait(barrier, len(peers))
+
+
+def node_kernel(nodes, own_ref, out_ref, local_sem, x_send, x_recv, c_send, c_recv):
+    node = lax.axis_index("node")
+    chips = nodes // 2
+    chip, core = node // 2, node % 2
+    sibling = chip * 2 + 1 - core
+    others = [lax.rem(chip + step, chips) * 2 + core for step in range(1, chips)]
+    greet([peer(node=other) for other in others] + [peer(node=sibling)])
+    chunks = own_ref.shape[0] // chunk_rows
+
+    keep = pltpu.make_async_copy(own_ref, out_ref.at[node], local_sem)
+    keep.start()
+
+    def to_chip(step, k):
+        rows = pl.ds(k * chunk_rows, chunk_rows)
+        return pltpu.make_async_remote_copy(
+            own_ref.at[rows], out_ref.at[node, rows], x_send.at[step - 1, k], x_recv.at[step - 1, k],
+            **peer(node=lax.rem(chip + step, chips) * 2 + core))
+
+    def to_core(step, k):
+        rows = pl.ds(k * chunk_rows, chunk_rows)
+        origin = lax.rem(chip - step + chips, chips) * 2 + core
+        source = own_ref.at[rows] if step == 0 else out_ref.at[origin, rows]
+        return pltpu.make_async_remote_copy(
+            source, out_ref.at[origin, rows], c_send.at[step, k], c_recv.at[step, k], **peer(node=sibling))
+
+    for k in range(chunks):
+        for step in range(1, chips):
+            to_chip(step, k).start()
+    for k in range(chunks):
+        to_core(0, k).start()
+    for k in range(chunks):
+        for step in range(1, chips):
+            to_chip(step, k).wait_recv()
+            to_core(step, k).start()
+    for k in range(chunks):
+        for step in range(1, chips):
+            to_chip(step, k).wait_send()
+        for step in range(chips):
+            to_core(step, k).wait()
+    keep.wait()
+
+
+def world_kernel(groups, nodes, own_ref, near_ref, act_ref, out_ref, act_out, local_sems,
+                 z_recv, right_send, left_send, x_send, x_recv, c_send, c_recv, a_send, a_recv):
+    mine, node = lax.axis_index("dp"), lax.axis_index("node")
+    chips = nodes // 2
+    chip, core = node // 2, node % 2
+    sibling = chip * 2 + 1 - core
+    greet([peer(dp=lax.rem(mine + step, groups)) for step in range(1, groups)]
+          + [peer(node=lax.rem(chip + step, chips) * 2 + core) for step in range(1, chips)]
+          + [peer(node=sibling)])
+    chunks = own_ref.shape[0] // chunk_rows
+    part = act_out.shape[2]
+
+    def hop(side, source, k, first):
+        rows = pl.ds(k * chunk_rows, chunk_rows)
+        sems = right_send if side > 0 else left_send
+        block = own_ref.at[rows] if first else out_ref.at[source, node, rows]
+        return pltpu.make_async_remote_copy(
+            block, out_ref.at[source, node, rows], sems.at[source, k], z_recv.at[source, k],
+            **peer(dp=mine + side))
+
+    def to_chip(source, step, k):
+        rows = pl.ds(k * chunk_rows, chunk_rows)
+        return pltpu.make_async_remote_copy(
+            out_ref.at[source, node, rows], out_ref.at[source, node, rows],
+            x_send.at[source, step - 1, k], x_recv.at[source, step - 1, k],
+            **peer(node=lax.rem(chip + step, chips) * 2 + core))
+
+    def to_core(source, step, k):
+        rows = pl.ds(k * chunk_rows, chunk_rows)
+        origin = lax.rem(chip - step + chips, chips) * 2 + core
+        return pltpu.make_async_remote_copy(
+            out_ref.at[source, origin, rows], out_ref.at[source, origin, rows],
+            c_send.at[source, step, k], c_recv.at[source, step, k], **peer(node=sibling))
+
+    def act_copy(step):
+        target = lax.rem(mine + step, groups)
+        columns = pl.ds(pl.multiple_of(target * part, part), part)
+        return pltpu.make_async_remote_copy(
+            act_ref.at[:, columns], act_out.at[mine], a_send.at[step - 1], a_recv.at[step - 1],
+            **peer(dp=target))
+
+    for k in range(chunks):
+        @pl.when(mine + 1 < groups)
+        def _():
+            hop(1, mine, k, True).start()
+
+        @pl.when(mine > 0)
+        def _():
+            hop(-1, mine, k, True).start()
+
+    keep_near = pltpu.make_async_copy(near_ref, out_ref.at[mine], local_sems.at[0])
+    keep_near.start()
+    own_columns = pl.ds(pl.multiple_of(mine * part, part), part)
+    keep_act = pltpu.make_async_copy(act_ref.at[:, own_columns], act_out.at[mine], local_sems.at[1])
+    keep_act.start()
+    for step in range(1, groups):
+        act_copy(step).start()
+
+    def sides(distance):
+        return (
+            (1, mine - distance, mine - distance >= 0, jnp.logical_and(mine - distance >= 0, mine + 1 < groups)),
+            (-1, mine + distance, mine + distance < groups, jnp.logical_and(mine + distance < groups, mine > 0)),
+        )
+
+    def spread(distance, k):
+        for side, source, here, further in sides(distance):
+            @pl.when(here)
+            def _():
+                hop(side, source, k, False).wait_recv()
+
+            @pl.when(further)
+            def _():
+                hop(side, source, k, False).start()
+
+            @pl.when(here)
+            def _():
+                for step in range(1, chips):
+                    to_chip(source, step, k).start()
+                to_core(source, 0, k).start()
+
+    def pass_on(distance, k):
+        for side, source, here, further in sides(distance):
+            @pl.when(here)
+            def _():
+                for step in range(1, chips):
+                    to_chip(source, step, k).wait_recv()
+                    to_core(source, step, k).start()
+
+    order = [(distance, k) for distance in range(1, groups) for k in range(chunks)]
+    for at, item in enumerate(order):
+        spread(*item)
+        if at >= 2:
+            pass_on(*order[at - 2])
+    for item in order[-2:]:
+        pass_on(*item)
+
+    for distance, k in order:
+        for side, source, here, further in sides(distance):
+            @pl.when(further)
+            def _():
+                hop(side, source, k, False).wait_send()
+
+            @pl.when(here)
+            def _():
+                for step in range(1, chips):
+                    to_chip(source, step, k).wait_send()
+                for step in range(chips):
+                    to_core(source, step, k).wait()
+    for k in range(chunks):
+        @pl.when(mine + 1 < groups)
+        def _():
+            hop(1, mine, k, True).wait_send()
+
+        @pl.when(mine > 0)
+        def _():
+            hop(-1, mine, k, True).wait_send()
+    for step in range(1, groups):
+        act_copy(step).wait()
+    keep_near.wait()
+    keep_act.wait()
+
+
+def anywhere(count):
+    return [pl.BlockSpec(memory_space=pl.ANY)] * count
+
+
+def gather_node(d_out, nodes):
+    chunks, chips = d_out.shape[0] // chunk_rows, nodes // 2
+    dma = pltpu.SemaphoreType.DMA
+    return pl.pallas_call(
+        functools.partial(node_kernel, nodes),
+        out_shape=jax.ShapeDtypeStruct((nodes,) + d_out.shape, d_out.dtype),
+        in_specs=anywhere(1),
+        out_specs=pl.BlockSpec(memory_space=pl.ANY),
+        scratch_shapes=[dma, dma((chips - 1, chunks)), dma((chips - 1, chunks)), dma((chips, chunks)), dma((chips, chunks))],
+        cost_estimate=pl.CostEstimate(flops=0, bytes_accessed=40 << 20, transcendentals=0),
+        compiler_params=pltpu.CompilerParams(collective_id=0, has_side_effects=True),
+    )(d_out)
+
+
+def gather_world(d_out, near, act, groups, nodes):
+    chunks, chips = d_out.shape[0] // chunk_rows, nodes // 2
+    dma = pltpu.SemaphoreType.DMA
+    return pl.pallas_call(
+        functools.partial(world_kernel, groups, nodes),
+        out_shape=(
+            jax.ShapeDtypeStruct((groups, nodes) + d_out.shape, d_out.dtype),
+            jax.ShapeDtypeStruct((groups, act.shape[0], act.shape[1] // groups), act.dtype),
+        ),
+        in_specs=anywhere(3),
+        out_specs=tuple(anywhere(2)),
+        scratch_shapes=[
+            dma((2,)), dma((groups, chunks)), dma((groups, chunks)), dma((groups, chunks)),
+            dma((groups, chips - 1, chunks)), dma((groups, chips - 1, chunks)),
+            dma((groups, chips, chunks)), dma((groups, chips, chunks)),
+            dma((groups - 1,)), dma((groups - 1,)),
+        ],
+        cost_estimate=pl.CostEstimate(flops=0, bytes_accessed=200 << 20, transcendentals=0),
+        compiler_params=pltpu.CompilerParams(collective_id=1, has_side_effects=True),
+    )(d_out, near, act)
+
+
+def routing(logits, groups):
+    scores = jax.nn.sigmoid(logits)
+    picked = (groups[..., None] == jnp.arange(logits.shape[1], dtype=jnp.int32)).astype(jnp.float32)
+    chosen = jnp.sum(picked * scores[:, None, :], axis=-1)
+    totals = jnp.sum(chosen, axis=-1, keepdims=True)
+    return picked, chosen, totals
+
+
+def gather_shards(d_out, logits, groups, slots, hidden_act, w_down):
+    dp_count, node_count = lax.axis_size("dp"), lax.axis_size("node")
+    me_dp, me_node, me_local = lax.axis_index("dp"), lax.axis_index("node"), lax.axis_index("local")
+    tokens, feat_local = d_out.shape
+    cap_rows, hid_units = hidden_act.shape[3], hidden_act.shape[4]
+    slot_count = node_count * cap_rows
+    group_tokens = node_count * tokens
+    act_rows = hidden_act.reshape(slot_count, hid_units)
+    weight = w_down.reshape(hid_units, feat_local)
+
+    picked, chosen, totals = routing(logits, groups)
+    gates = (route_scale * chosen / totals).astype(jnp.bfloat16).astype(jnp.float32)
+    pairs = jnp.concatenate([groups.astype(jnp.float32), slots.astype(jnp.float32), gates], axis=1).T
+    pairs = jnp.concatenate([pairs, jnp.zeros((2, tokens), jnp.float32)], axis=0)
+    near = gather_node(d_out, node_count)
+    facts = lax.all_gather(pairs, ("dp", "node"), axis=0, tiled=False)
+    facts = facts.reshape(dp_count, node_count, 8, tokens)
+    expert = me_node.astype(jnp.float32)
+    live = (facts[:, :, 0:2] == expert) & (facts[:, :, 2:4] >= 0)
+    source = jnp.arange(node_count, dtype=jnp.float32)[None, :, None, None] * cap_rows
+    where = jnp.sum(jnp.where(live, facts[:, :, 2:4] + source + 1.0, 0.0), axis=2) - 1.0
+    where = where.reshape(dp_count, group_tokens).astype(jnp.int32)
+    gate = jnp.sum(jnp.where(live, facts[:, :, 4:6], 0.0), axis=2).reshape(dp_count, group_tokens)
+
+    own_where = lax.dynamic_index_in_dim(where, me_dp, 0, keepdims=False)
+    own_gate = lax.dynamic_index_in_dim(gate, me_dp, 0, keepdims=False)
+    fills = jnp.arange(slot_count, dtype=jnp.int32)[:, None] == own_where[None, :]
+    rows = jnp.dot(
+        fills.astype(jnp.bfloat16), near.reshape(group_tokens, feat_local), preferred_element_type=jnp.float32
+    ).astype(jnp.bfloat16)
+    row_gate = jnp.sum(jnp.where(fills, own_gate[None, :], 0.0), axis=1)
+    term = lax.dot_general(rows, weight, (((1,), (1,)), ((), ())), preferred_element_type=jnp.float32)
+    dot_part = jnp.sum(act_rows.astype(jnp.float32) * term, axis=1)
+    half = hid_units // 2
+    gated = row_gate[:, None] * term
+    away = lax.dynamic_slice_in_dim(gated, (1 - me_local) * half, half, axis=1).astype(jnp.bfloat16)
+    home = lax.dynamic_slice_in_dim(gated, me_local * half, half, axis=1)
+    come = lax.ppermute(away, "local", [(0, 1), (1, 0)])
+    d_hidden = (home + come.astype(jnp.float32)).astype(jnp.bfloat16)
+    d_hidden = d_hidden.reshape(1, 1, node_count, cap_rows, half)
+
+    token_dot = jnp.sum(jnp.where(fills, dot_part[:, None], 0.0), axis=0)
+    is_mine = (jnp.arange(node_count) == me_node)[:, None]
+    all_dots = lax.psum(jnp.where(is_mine, token_dot[None, :], 0.0), ("node", "local"))
+
+    world, acts = gather_world(d_out, near, act_rows, dp_count, node_count)
+    spots = (where[:, :, None] == jnp.arange(slot_count, dtype=jnp.int32)).astype(jnp.bfloat16)
+    spots = spots * gate.astype(jnp.bfloat16)[:, :, None]
+    left = jnp.einsum("dtc,dch->dth", spots, acts, preferred_element_type=jnp.float32).astype(jnp.bfloat16)
+    d_wdown = lax.dot_general(
+        left.reshape(dp_count * group_tokens, -1), world.reshape(dp_count * group_tokens, feat_local),
+        (((0,), (0,)), ((), ())), preferred_element_type=jnp.float32,
+    ).astype(jnp.bfloat16)
+    d_wdown = d_wdown.reshape((1,) + d_wdown.shape)
+
+    my_dots = lax.dynamic_slice_in_dim(all_dots, me_node * tokens, tokens, axis=1).T
+    route_dot = jnp.sum(picked * my_dots[:, None, :], axis=-1)
+    return (logit_grads(picked, chosen, totals, route_dot), d_hidden, d_wdown)
+
+
+def logit_grads(picked, chosen, totals, route_dot):
+    mean_dot = jnp.sum(chosen / totals * route_dot, axis=-1, keepdims=True)
+    d_chosen = route_scale * (route_dot - mean_dot) / totals
+    return jnp.sum(picked * (d_chosen * chosen * (1.0 - chosen))[..., None], axis=1)
 
 
 def shards(d_out, logits, groups, slots, hidden_act, w_down):
@@ -80,4 +375,11 @@
         P("dp", "node", None, None, "local"),
         P("node", "dp", "local"),
     )
-    return jax.shard_map(shards, mesh=mesh, in_specs=in_specs, out_specs=out_specs, check_vma=False)
+
+    def run(d_out, *rest):
+        gathered = d_out.shape[0] * d_out.shape[1] // mesh.shape["local"] * d_out.dtype.itemsize
+        fits = gathered <= gather_limit and mesh.shape["local"] == 2 and rest[0].shape[1] == mesh.shape["node"]
+        body = gather_shards if fits else shards
+        return jax.shard_map(body, mesh=mesh, in_specs=in_specs, out_specs=out_specs, check_vma=False)(d_out, *rest)
+
+    return run

time: 228 us -> 214 us (0.939)
  waiting for transfers between devices: 166 us -> 0.01 us
  Pallas kernels: 0 us -> 149 us
  blocking collectives: 11.9 us -> 36 us
  between operations: 14.1 us -> 0.8 us
  starting transfers between devices: 7.64 us -> 1.58 us
  local copies, waits for them, and re-layouts: 5.57 us -> 0.11 us
    pallas_call x0 -> x2, Pallas kernels: none -> 149 us  [the longest x1 120 us: gather_world(): pl.pallas_call(functools.partial(world_kernel, groups, nodes), out_shape=...]
    reduce_scatter x2 -> x0, waiting for transfers between devices: 137 us -> none  [the longest x1 122 us: shards(): lax.psum_scatter(weight_term.astype(jnp.bfloat16), 'dp', scatter_dimensio...]
    all_to_all x2 -> x0, waiting for transfers between devices: 28.9 us -> none  [the longest x1 25.3 us: shards(): lax.all_to_all(send_rows, 'node', split_axis=0, concat_axis=0, tiled=True)]
    all_gather x0 -> x1, blocking collectives: none -> 23.2 us  [gather_shards(): facts = lax.all_gather(pairs, ('dp', 'node'), axis=0, tiled=False)]
    all_to_all x2 -> x0, starting transfers between devices: 7.56 us -> none  [the longest x1 4.34 us: shards(): lax.all_to_all(send_rows, 'node', split_axis=0, concat_axis=0, tiled=True)]
    psum x1, blocking collectives: 5.79 us -> 12.8 us  [gather_shards(): lax.psum(jnp.where(is_mine, token_dot[None, :], 0.0), ('node', 'local'))]
    all_to_all x1 -> x0, blocking collectives: 6.08 us -> none  [shards(): lax.all_to_all(send_gates, 'node', split_axis=0, concat_axis=0, tiled=True)]
    unnamed x9 -> x7, local copies, waits for them, and re-layouts: 4.71 us -> 0.02 us
  transfers between devices with their start and end apart: 4 -> 1, of which waited for: 4 -> 0; matrix products, arithmetic and copies ran while one was open for 5% -> 6% of each run, Pallas kernels for 0% -> 56%
where the time goes in v1:
time: 214 us
  Pallas kernels  149 us (70%)
  blocking collectives  36 us (17%)
  matrix products  21.1 us (10%)
  other arithmetic  4.81 us (2%)
    pallas_call x1, Pallas kernels, gather_world(): pl.pallas_call(functools.partial(world_kernel, groups, nodes), out_shape=...  120 us
    pallas_call x1, Pallas kernels, gather_node(): pl.pallas_call(functools.partial(node_kernel, nodes), out_shape=jax.Shape...  29.5 us
    all_gather x1, blocking collectives, gather_shards(): facts = lax.all_gather(pairs, ('dp', 'node'), axis=0, tiled=False)  23.2 us
    psum x1, blocking collectives, gather_shards(): lax.psum(jnp.where(is_mine, token_dot[None, :], 0.0), ('node', 'local'))  12.8 us
    dot_general x1, matrix products, gather_shards(): lax.dot_general(left.reshape(dp_count * group_tokens, -1), world.reshape(...  10.3 us
    dot_general x1, matrix products, gather_shards(): lax.dot_general(rows, weight, (((1,), (1,)), ((), ())), preferred_element...  5.52 us
  transfers between devices with their start and end apart: 1, of which 0 were waited for; matrix products, arithmetic and copies ran while one was open for 6% of the time, Pallas kernels for 56%

profile of v1, /device:TPU:0, one launch (start us, length us, event | category | flops | bytes accessed | tf_op | source)
XLA Modules:
  0.0 213.8 jit_solution(8304681579748612655)
XLA Ops:
  0.7 0.7 convert_element_type.57
  1.3 0.7 convert_element_type.56
  2.0 0.7 add_divide_fusion
  2.7 0.7 select_reduce_fusion.3
  3.5 23.2 %all-gather = f32[128,128]{1,0:T(8,128)S(1)} all-gather(f32[8,128]{1,0:T(8,128)S(1)} %concatenate.7), channel_id=2, replica_groups=mesh['dp'=4,'node'=4,'local'=2] {'dp','node'}, dimensions={0}, use_global_device_ids=true | all-gather | bytes 69632 | tf_op jit(solution)/shard_map/all_gather | solution.py:253
  26.7 0.1 fusion.9
  26.9 29.5 %shard_map.85.near_ref = bf16[4,128,3584]{2,1,0:T(8,128)(2,1)} custom-call(bf16[128,3584]{1,0:T(8,128)(2,1)} %own_ref.3), custom_call_target="tpu_custom_call" | custom-call | bytes 41943040 | tf_op jit(solution)/shard_map/pallas_call | solution.py:197
  56.4 0.0 copy-start
  56.4 3.3 %convolution_convert_fusion = bf16[288,3584]{1,0:T(8,128)(2,1)S(1)} fusion(bf16[512,3584]{1,0:T(8,128)(2,1)} %bitcast.37, s32[512]{0:T(512)S(1)} %bitcast.49), kind=kOutput, calls=%fused_computation.2 | convolution fusion | flops 1058144256 | bytes 5736448 | tf_op jit(solution)/shard_map/dot_general | solution.py:265
  59.7 0.0 copy-done
  59.8 5.5 %multiply_reduce_fusion = (f32[288]{0:T(512)S(1)}, f32[288,1024]{1,0:T(8,128)S(1)}) fusion(bf16[288,1024]{1,0:T(8,128)(2,1)S(1)} %bitcast.40, bf16[288,3584]{1,0:T(8,128)(2,1)S(1)} %convolution_convert_fusion, bf16[1,1024,3584]{2,1,0:T(8,128)(2,1)} %param.11), kind=kOutput, calls=%fused_computation.9 | convolution fusion | flops 2114813696 | bytes 11175040 | tf_op jit(solution)/shard_map/dot_general | solution.py:269
  65.3 0.2 select_reduce_fusion
  65.5 0.1 broadcast_multiply_fusion
  65.7 1.6 collective-permute-start
  67.3 0.0 copy-start.1
  67.3 119.9 %shard_map.86 = (bf16[4,4,128,3584]{3,2,1,0:T(8,128)(2,1)}, bf16[4,288,256]{2,1,0:T(8,128)(2,1)}) custom-call(bf16[128,3584]{1,0:T(8,128)(2,1)} %own_ref.3, bf16[4,128,3584]{2,1,0:T(8,128)(2,1)} %shard_map.85.near_ref, bf16[288,1024]{1,0:T(8,128)(2,1)} %bitcast.39), custom_call_target="tpu_custom_call" | custom-call | bytes 209715200 | tf_op jit(solution)/shard_map/pallas_call | solution.py:211
  187.2 0.1 broadcast_select_fusion
  187.3 12.8 %psum.7 = f32[4,512]{1,0:T(4,128)S(1)} all-reduce(f32[4,512]{1,0:T(4,128)S(1)} %broadcast_select_fusion), channel_id=1, replica_groups=mesh['dp'=4,'node'=4,'local'=2] {'node','local'}, use_global_device_ids=true, to_apply=%region_5.6 | all-reduce | flops 2048 | bytes 16384 | tf_op jit(solution)/shard_map/psum | solution.py:281
  200.1 0.0 copy-done.1
  200.1 1.9 convolution_convert_fusion.2
  202.0 10.3 %fusion.2 = bf16[1,256,3584]{2,1,0:T(8,128)(2,1)} fusion(bf16[2048,256]{1,0:T(8,128)(2,1)S(1)} %bitcast.38, bf16[2048,3584]{1,0:T(8,128)(2,1)} %bitcast.36), kind=kOutput, calls=%fused_computation.4 | convolution fusion | flops 3759013888 | bytes 17563648 | tf_op jit(solution)/shard_map/dot_general | solution.py:287
  212.4 0.6 select_reduce_fusion.5
  213.0 0.0 collective-permute-done
  213.0 0.8 add_convert_fusion
  (16 shorter events, 0.2 us)
Async XLA Ops:
  56.4 3.4 %copy-start = (bf16[1,1,4,72,1024]{4,3,2,1,0:T(8,128)(2,1)S(1)}, bf16[1,1,4,72,1024]{4,3,2,1,0:T(8,128)(2,1)}, u32[]{:S(2)}) copy-start(bf16[1,1,4,72,1024]{4,3,2,1,0:T(8,128)(2,1)} %param.10) | copy-start | bytes 1769476
  65.7 147.2 %collective-permute-start = (bf16[288,512]{1,0:T(8,128)(2,1)S(1)}, bf16[288,512]{1,0:T(8,128)(2,1)S(1)}, u32[]{:S(2)}, u32[]{:S(2)}) collective-permute-start(bf16[288,512]{1,0:T(8,128)(2,1)S(1)} %dynamic-slice_convert_fusion), channel_id=1, source_target_pairs={{0,1},{1,0},{2,3},{3,2},{4,5},{5,4},{6,7},{7,6},{8,9},{9,8},{10,11... | collective-permute-start | bytes 884744 | tf_op jit(solution)/shard_map/ppermute | solution.py:275
  67.3 132.8 %copy-start.1 = (s32[128,2]{0,1:T(2,128)S(1)}, s32[128,2]{0,1:T(2,128)}, u32[]{:S(2)}) copy-start(s32[128,2]{0,1:T(2,128)} %param.8) | copy-start | bytes 3076

commit v2 on v1

--- a/solution.py
+++ b/solution.py
@@ -10,6 +10,7 @@
 route_scale = 2.5
 gather_limit = 20 * 1024 * 1024
 chunk_rows = 32
+pass_lag = 3
 
 
 def peer(**where):
@@ -23,80 +24,43 @@
     pl.semaphore_wait(barrier, len(peers))
 
 
-def node_kernel(nodes, own_ref, out_ref, local_sem, x_send, x_recv, c_send, c_recv):
-    node = lax.axis_index("node")
-    chips = nodes // 2
-    chip, core = node // 2, node % 2
-    sibling = chip * 2 + 1 - core
-    others = [lax.rem(chip + step, chips) * 2 + core for step in range(1, chips)]
-    greet([peer(node=other) for other in others] + [peer(node=sibling)])
-    chunks = own_ref.shape[0] // chunk_rows
-
-    keep = pltpu.make_async_copy(own_ref, out_ref.at[node], local_sem)
-    keep.start()
-
-    def to_chip(step, k):
-        rows = pl.ds(k * chunk_rows, chunk_rows)
-        return pltpu.make_async_remote_copy(
-            own_ref.at[rows], out_ref.at[node, rows], x_send.at[step - 1, k], x_recv.at[step - 1, k],
-            **peer(node=lax.rem(chip + step, chips) * 2 + core))
-
-    def to_core(step, k):
-        rows = pl.ds(k * chunk_rows, chunk_rows)
-        origin = lax.rem(chip - step + chips, chips) * 2 + core
-        source = own_ref.at[rows] if step == 0 else out_ref.at[origin, rows]
-        return pltpu.make_async_remote_copy(
-            source, out_ref.at[origin, rows], c_send.at[step, k], c_recv.at[step, k], **peer(node=sibling))
-
-    for k in range(chunks):
-        for step in range(1, chips):
-            to_chip(step, k).start()
-    for k in range(chunks):
-        to_core(0, k).start()
-    for k in range(chunks):
-        for step in range(1, chips):
-            to_chip(step, k).wait_recv()
-            to_core(step, k).start()
-    for k in range(chunks):
-        for step in range(1, chips):
-            to_chip(step, k).wait_send()
-        for step in range(chips):
-            to_core(step, k).wait()
-    keep.wait()
-
-
-def world_kernel(groups, nodes, own_ref, near_ref, act_ref, out_ref, act_out, local_sems,
-                 z_recv, right_send, left_send, x_send, x_recv, c_send, c_recv, a_send, a_recv):
+def world_kernel(groups, nodes, own_ref, act_ref, facts_ref, out_ref, act_out, facts_out, stage, local_sems,
+                 z_recv, right_send, left_send, x_send, x_recv, c_send, c_recv, a_send, a_recv, f_send, f_recv):
     mine, node = lax.axis_index("dp"), lax.axis_index("node")
     chips = nodes // 2
     chip, core = node // 2, node % 2
     sibling = chip * 2 + 1 - core
-    greet([peer(dp=lax.rem(mine + step, groups)) for step in range(1, groups)]
-          + [peer(node=lax.rem(chip + step, chips) * 2 + core) for step in range(1, chips)]
-          + [peer(node=sibling)])
+    world = groups * nodes
+    everyone = []
+    for step in range(1, world):
+        other = lax.rem(mine * nodes + node + step, world)
+        everyone.append(peer(dp=other // nodes, node=other % nodes))
+    greet(everyone)
     chunks = own_ref.shape[0] // chunk_rows
     part = act_out.shape[2]
 
+    def block(source, origin, k):
+        return out_ref.at[source, origin, pl.ds(k * chunk_rows, chunk_rows)]
+
+    def own(k):
+        return own_ref.at[pl.ds(k * chunk_rows, chunk_rows)]
+
     def hop(side, source, k, first):
-        rows = pl.ds(k * chunk_rows, chunk_rows)
         sems = right_send if side > 0 else left_send
-        block = own_ref.at[rows] if first else out_ref.at[source, node, rows]
-        return pltpu.make_async_remote_copy(
-            block, out_ref.at[source, node, rows], sems.at[source, k], z_recv.at[source, k],
-            **peer(dp=mine + side))
-
-    def to_chip(source, step, k):
-        rows = pl.ds(k * chunk_rows, chunk_rows)
-        return pltpu.make_async_remote_copy(
-            out_ref.at[source, node, rows], out_ref.at[source, node, rows],
+        return pltpu.make_async_remote_copy(
+            own(k) if first else block(source, node, k), block(source, node, k),
+            sems.at[source, k], z_recv.at[source, k], **peer(dp=mine + side))
+
+    def to_chip(source, step, k, first):
+        return pltpu.make_async_remote_copy(
+            own(k) if first else block(source, node, k), block(source, node, k),
             x_send.at[source, step - 1, k], x_recv.at[source, step - 1, k],
             **peer(node=lax.rem(chip + step, chips) * 2 + core))
 
-    def to_core(source, step, k):
-        rows = pl.ds(k * chunk_rows, chunk_rows)
+    def to_core(source, step, k, first):
         origin = lax.rem(chip - step + chips, chips) * 2 + core
         return pltpu.make_async_remote_copy(
-            out_ref.at[source, origin, rows], out_ref.at[source, origin, rows],
+            own(k) if first and step == 0 else block(source, origin, k), block(source, origin, k),
             c_send.at[source, step, k], c_recv.at[source, step, k], **peer(node=sibling))
 
     def act_copy(step):
@@ -106,22 +70,9 @@
             act_ref.at[:, columns], act_out.at[mine], a_send.at[step - 1], a_recv.at[step - 1],
             **peer(dp=target))
 
-    for k in range(chunks):
-        @pl.when(mine + 1 < groups)
-        def _():
-            hop(1, mine, k, True).start()
-
-        @pl.when(mine > 0)
-        def _():
-            hop(-1, mine, k, True).start()
-
-    keep_near = pltpu.make_async_copy(near_ref, out_ref.at[mine], local_sems.at[0])
-    keep_near.start()
-    own_columns = pl.ds(pl.multiple_of(mine * part, part), part)
-    keep_act = pltpu.make_async_copy(act_ref.at[:, own_columns], act_out.at[mine], local_sems.at[1])
-    keep_act.start()
-    for step in range(1, groups):
-        act_copy(step).start()
+    def fact_copy(step):
+        return pltpu.make_async_remote_copy(
+            facts_ref, facts_out.at[mine, node], f_send.at[step - 1], f_recv.at[step - 1], **everyone[step - 1])
 
     def sides(distance):
         return (
@@ -130,6 +81,15 @@
         )
 
     def spread(distance, k):
+        if distance == 0:
+            for side, source, here, further in sides(0):
+                @pl.when(further)
+                def _():
+                    hop(side, source, k, True).start()
+            for step in range(1, chips):
+                to_chip(mine, step, k, True).start()
+            to_core(mine, 0, k, True).start()
+            return
         for side, source, here, further in sides(distance):
             @pl.when(here)
             def _():
@@ -142,70 +102,70 @@
             @pl.when(here)
             def _():
                 for step in range(1, chips):
-                    to_chip(source, step, k).start()
-                to_core(source, 0, k).start()
+                    to_chip(source, step, k, False).start()
+                to_core(source, 0, k, False).start()
 
     def pass_on(distance, k):
-        for side, source, here, further in sides(distance):
+        for side, source, here, further in sides(distance)[:1 if distance == 0 else 2]:
             @pl.when(here)
             def _():
                 for step in range(1, chips):
-                    to_chip(source, step, k).wait_recv()
-                    to_core(source, step, k).start()
-
-    order = [(distance, k) for distance in range(1, groups) for k in range(chunks)]
-    for at, item in enumerate(order):
-        spread(*item)
-        if at >= 2:
-            pass_on(*order[at - 2])
-    for item in order[-2:]:
-        pass_on(*item)
+                    to_chip(source, step, k, distance == 0).wait_recv()
+                    to_core(source, step, k, distance == 0).start()
+
+    fetch = pltpu.make_async_copy(own_ref, stage, local_sems.at[0])
+    fetch.start()
+    own_columns = pl.ds(pl.multiple_of(mine * part, part), part)
+    keep_act = pltpu.make_async_copy(act_ref.at[:, own_columns], act_out.at[mine], local_sems.at[1])
+    keep_act.start()
+    keep_facts = pltpu.make_async_copy(facts_ref, facts_out.at[mine, node], local_sems.at[2])
+    keep_facts.start()
+    for k in range(chunks):
+        spread(0, k)
+    for step in range(1, groups):
+        act_copy(step).start()
+    for step in range(1, world):
+        fact_copy(step).start()
+    fetch.wait()
+    keep = pltpu.make_async_copy(stage, out_ref.at[mine, node], local_sems.at[0])
+    keep.start()
+
+    order = [(distance, k) for distance in range(groups) for k in range(chunks)]
+    for at in range(chunks, len(order) + pass_lag):
+        if at < len(order):
+            spread(*order[at])
+        if at == chunks:
+            for item in order[:chunks - pass_lag]:
+                pass_on(*item)
+        pass_on(*order[at - pass_lag])
 
     for distance, k in order:
         for side, source, here, further in sides(distance):
             @pl.when(further)
             def _():
-                hop(side, source, k, False).wait_send()
-
+                hop(side, source, k, distance == 0).wait_send()
+
+        for side, source, here, further in sides(distance)[:1 if distance == 0 else 2]:
             @pl.when(here)
             def _():
                 for step in range(1, chips):
-                    to_chip(source, step, k).wait_send()
+                    to_chip(source, step, k, distance == 0).wait_send()
                 for step in range(chips):
-                    to_core(source, step, k).wait()
-    for k in range(chunks):
-        @pl.when(mine + 1 < groups)
-        def _():
-            hop(1, mine, k, True).wait_send()
-
-        @pl.when(mine > 0)
-        def _():
-            hop(-1, mine, k, True).wait_send()
+                    to_core(source, step, k, distance == 0).wait()
     for step in range(1, groups):
         act_copy(step).wait()
-    keep_near.wait()
+    for step in range(1, world):
+        fact_copy(step).wait()
+    keep.wait()
     keep_act.wait()
+    keep_facts.wait()
 
 
 def anywhere(count):
     return [pl.BlockSpec(memory_space=pl.ANY)] * count
 
 
-def gather_node(d_out, nodes):
-    chunks, chips = d_out.shape[0] // chunk_rows, nodes // 2
-    dma = pltpu.SemaphoreType.DMA
-    return pl.pallas_call(
-        functools.partial(node_kernel, nodes),
-        out_shape=jax.ShapeDtypeStruct((nodes,) + d_out.shape, d_out.dtype),
-        in_specs=anywhere(1),
-        out_specs=pl.BlockSpec(memory_space=pl.ANY),
-        scratch_shapes=[dma, dma((chips - 1, chunks)), dma((chips - 1, chunks)), dma((chips, chunks)), dma((chips, chunks))],
-        cost_estimate=pl.CostEstimate(flops=0, bytes_accessed=40 << 20, transcendentals=0),
-        compiler_params=pltpu.CompilerParams(collective_id=0, has_side_effects=True),
-    )(d_out)
-
-
-def gather_world(d_out, near, act, groups, nodes):
+def gather_world(d_out, act, facts, groups, nodes):
     chunks, chips = d_out.shape[0] // chunk_rows, nodes // 2
     dma = pltpu.SemaphoreType.DMA
     return pl.pallas_call(
@@ -213,18 +173,21 @@
         out_shape=(
             jax.ShapeDtypeStruct((groups, nodes) + d_out.shape, d_out.dtype),
             jax.ShapeDtypeStruct((groups, act.shape[0], act.shape[1] // groups), act.dtype),
+            jax.ShapeDtypeStruct((groups, nodes) + facts.shape, facts.dtype),
         ),
         in_specs=anywhere(3),
-        out_specs=tuple(anywhere(2)),
+        out_specs=tuple(anywhere(3)),
         scratch_shapes=[
-            dma((2,)), dma((groups, chunks)), dma((groups, chunks)), dma((groups, chunks)),
+            pltpu.VMEM(d_out.shape, d_out.dtype),
+            dma((3,)), dma((groups, chunks)), dma((groups, chunks)), dma((groups, chunks)),
             dma((groups, chips - 1, chunks)), dma((groups, chips - 1, chunks)),
             dma((groups, chips, chunks)), dma((groups, chips, chunks)),
             dma((groups - 1,)), dma((groups - 1,)),
+            dma((groups * nodes - 1,)), dma((groups * nodes - 1,)),
         ],
         cost_estimate=pl.CostEstimate(flops=0, bytes_accessed=200 << 20, transcendentals=0),
-        compiler_params=pltpu.CompilerParams(collective_id=1, has_side_effects=True),
-    )(d_out, near, act)
+        compiler_params=pltpu.CompilerParams(collective_id=0, has_side_effects=True),
+    )(d_out, act, facts)
 
 
 def routing(logits, groups):
@@ -249,9 +212,9 @@
     gates = (route_scale * chosen / totals).astype(jnp.bfloat16).astype(jnp.float32)
     pairs = jnp.concatenate([groups.astype(jnp.float32), slots.astype(jnp.float32), gates], axis=1).T
     pairs = jnp.concatenate([pairs, jnp.zeros((2, tokens), jnp.float32)], axis=0)
-    near = gather_node(d_out, node_count)
-    facts = lax.all_gather(pairs, ("dp", "node"), axis=0, tiled=False)
-    facts = facts.reshape(dp_count, node_count, 8, tokens)
+    world, acts, facts = gather_world(d_out, act_rows, pairs, dp_count, node_count)
+    world = world.reshape(dp_count, group_tokens, feat_local)
+    near = lax.dynamic_index_in_dim(world, me_dp, 0, keepdims=False)
     expert = me_node.astype(jnp.float32)
     live = (facts[:, :, 0:2] == expert) & (facts[:, :, 2:4] >= 0)
     source = jnp.arange(node_count, dtype=jnp.float32)[None, :, None, None] * cap_rows
@@ -263,7 +226,7 @@
     own_gate = lax.dynamic_index_in_dim(gate, me_dp, 0, keepdims=False)
     fills = jnp.arange(slot_count, dtype=jnp.int32)[:, None] == own_where[None, :]
     rows = jnp.dot(
-        fills.astype(jnp.bfloat16), near.reshape(group_tokens, feat_local), preferred_element_type=jnp.float32
+        fills.astype(jnp.bfloat16), near, preferred_element_type=jnp.float32
     ).astype(jnp.bfloat16)
     row_gate = jnp.sum(jnp.where(fills, own_gate[None, :], 0.0), axis=1)
     term = lax.dot_general(rows, weight, (((1,), (1,)), ((), ())), preferred_element_type=jnp.float32)
@@ -277,10 +240,17 @@
     d_hidden = d_hidden.reshape(1, 1, node_count, cap_rows, half)
 
     token_dot = jnp.sum(jnp.where(fills, dot_part[:, None], 0.0), axis=0)
-    is_mine = (jnp.arange(node_count) == me_node)[:, None]
-    all_dots = lax.psum(jnp.where(is_mine, token_dot[None, :], 0.0), ("node", "local"))
-
-    world, acts = gather_world(d_out, near, act_rows, dp_count, node_count)
+    parts = token_dot.reshape(node_count, tokens)
+    kept = lax.dynamic_slice_in_dim(parts, me_node, 1, axis=0)
+    my_dots = jnp.where(jnp.arange(node_count)[:, None] == me_node, kept, 0.0)
+    members = node_count * 2
+    me = me_node * 2 + me_local
+    for step in range(1, members):
+        target, origin = lax.rem(me + step, members), lax.rem(me - step + members, members)
+        sent = lax.dynamic_slice_in_dim(parts, target // 2, 1, axis=0)
+        got = lax.ppermute(sent, ("node", "local"), [(i, (i + step) % members) for i in range(members)])
+        my_dots = my_dots + jnp.where(jnp.arange(node_count)[:, None] == origin // 2, got, 0.0)
+
     spots = (where[:, :, None] == jnp.arange(slot_count, dtype=jnp.int32)).astype(jnp.bfloat16)
     spots = spots * gate.astype(jnp.bfloat16)[:, :, None]
     left = jnp.einsum("dtc,dch->dth", spots, acts, preferred_element_type=jnp.float32).astype(jnp.bfloat16)
@@ -290,7 +260,7 @@
     ).astype(jnp.bfloat16)
     d_wdown = d_wdown.reshape((1,) + d_wdown.shape)
 
-    my_dots = lax.dynamic_slice_in_dim(all_dots, me_node * tokens, tokens, axis=1).T
+    my_dots = my_dots.T
     route_dot = jnp.sum(picked * my_dots[:, None, :], axis=-1)
     return (logit_grads(picked, chosen, totals, route_dot), d_hidden, d_wdown)
 

time: 214 us -> 133 us (0.62)
  Pallas kernels: 149 us -> 90.4 us
  blocking collectives: 36 us -> 0 us
  waiting for transfers between devices: 0.01 us -> 7.74 us
  starting transfers between devices: 1.58 us -> 8.11 us
  matrix products: 21.1 us -> 18.9 us
    pallas_call x1 -> x0, Pallas kernels: 29.5 us -> none  [gather_node(): pl.pallas_call(functools.partial(node_kernel, nodes), out_shape=jax.Shape...]
    pallas_call x1, Pallas kernels: 120 us -> 90.4 us  [gather_world(): pl.pallas_call(functools.partial(world_kernel, groups, nodes), out_shape=...]
    all_gather x1 -> x0, blocking collectives: 23.2 us -> none  [gather_shards(): facts = lax.all_gather(pairs, ('dp', 'node'), axis=0, tiled=False)]
    psum x1 -> x0, blocking collectives: 12.8 us -> none  [gather_shards(): lax.psum(jnp.where(is_mine, token_dot[None, :], 0.0), ('node', 'local'))]
    ppermute x0 -> x7, starting transfers between devices: none -> 6.88 us  [gather_shards(): lax.ppermute(sent, ('node', 'local'), [(i, (i + step) % members) for i in...]
    ppermute x1, waiting for transfers between devices: 0.01 us -> 5.76 us  [gather_shards(): come = lax.ppermute(away, 'local', [(0, 1), (1, 0)])]
    dot_general x1 -> x0, matrix products: 3.34 us -> none  [gather_shards(): jnp.dot(fills.astype(jnp.bfloat16), near.reshape(group_tokens, feat_local...]
    dot_general x1, matrix products: 5.52 us -> 7.74 us  [gather_shards(): lax.dot_general(rows, weight, (((1,), (1,)), ((), ())), preferred_element...]
  transfers between devices with their start and end apart: 1 -> 8, of which waited for: 0 -> 3; matrix products, arithmetic and copies ran while one was open for 6% -> 9% of each run, Pallas kernels for 56% -> 0%
where the time goes in v2:
time: 133 us
  Pallas kernels  90.4 us (68%)
  matrix products  18.9 us (14%)
  starting transfers between devices  8.11 us (6%)
  waiting for transfers between devices  7.74 us (6%)
  other arithmetic  5.79 us (4%)
    pallas_call x1, Pallas kernels, gather_world(): pl.pallas_call(functools.partial(world_kernel, groups, nodes), out_shape=...  90.4 us
    dot_general x1, matrix products, gather_shards(): lax.dot_general(left.reshape(dp_count * group_tokens, -1), world.reshape(...  10.3 us
    dot_general x1, matrix products, gather_shards(): lax.dot_general(rows, weight, (((1,), (1,)), ((), ())), preferred_element...  7.74 us
    ppermute x7, starting transfers between devices, gather_shards(): lax.ppermute(sent, ('node', 'local'), [(i, (i + step) % members) for i in...  6.88 us
    ppermute x1, waiting for transfers between devices, gather_shards(): come = lax.ppermute(away, 'local', [(0, 1), (1, 0)])  5.76 us
  transfers between devices with their start and end apart: 8, of which 3 were waited for; matrix products, arithmetic and copies ran while one was open for 9% of the time, Pallas kernels for 0%

profile of v2, /device:TPU:0, one launch (start us, length us, event | category | flops | bytes accessed | tf_op | source)
XLA Modules:
  0.0 132.6 jit_solution(305873171936883634)
XLA Ops:
  0.8 0.7 convert_element_type.57
  1.5 0.7 convert_element_type.56
  2.2 0.7 add_divide_fusion
  2.9 0.7 select_reduce_fusion.4
  3.6 0.6 concatenate.7.facts_ref
  4.2 90.4 %shard_map.85 = (bf16[4,4,128,3584]{3,2,1,0:T(8,128)(2,1)}, bf16[4,288,256]{2,1,0:T(8,128)(2,1)}, f32[4,4,8,128]{3,2,1,0:T(8,128)}) custom-call(bf16[128,3584]{1,0:T(8,128)(2,1)} %own_ref.1, bf16[288,1024]{1,0:T(8,128)(2,1)} %bitcast.51, f32[8,128]{1,0:T(8,128)} %concatenate.7.facts_ref), custom_call_target="tpu_custom_call" | custom-call | bytes 209715200 | tf_op jit(solution)/shard_map/pallas_call | solution.py:171
  94.7 1.1 select_reduce_fusion.2
  95.8 0.0 copy-start.1
  95.8 7.7 %multiply_reduce_fusion = (f32[288]{0:T(512)S(1)}, f32[288,1024]{1,0:T(8,128)S(1)}) fusion(bf16[288,1024]{1,0:T(8,128)(2,1)} %bitcast.52, bf16[1,1024,3584]{2,1,0:T(8,128)(2,1)} %param.11, bf16[4,512,3584]{2,1,0:T(8,128)(2,1)} %bitcast.48, s32[]{:T(128)S(6)} %select_n.149, s32[512]{0:T(512)S(1)} %bitcast.61), kind=kOutput, calls=%fused_computation.11 | convolution fusion | flops 3172957952 | bytes 12782724 | tf_op jit(solution)/shard_map/dot_general | solution.py:232
  103.6 0.2 select_reduce_fusion
  103.8 2.5 %collective-permute-start.6 = (f32[1,128]{1,0:T(1,128)S(1)}, f32[1,128]{1,0:T(1,128)S(1)}, u32[]{:S(2)}, u32[]{:S(2)}) collective-permute-start(f32[1,128]{1,0:T(1,128)S(1)} %get-tuple-element.16), channel_id=1, source_target_pairs={{0,7},{1,0},{2,1},{3,2},{4,3},{5,4},{6,5},{7,6},{8,15},{9,8},{10,9... | collective-permute-start | bytes 1544 | tf_op jit(solution)/shard_map/ppermute | solution.py:251
  106.3 0.3 collective-permute-start.5
  106.6 0.5 collective-permute-start.4
  107.1 1.5 %collective-permute-start.3 = (f32[1,128]{1,0:T(1,128)S(1)}, f32[1,128]{1,0:T(1,128)S(1)}, u32[]{:S(2)}, u32[]{:S(2)}) collective-permute-start(f32[1,128]{1,0:T(1,128)S(1)} %get-tuple-element.19), channel_id=1, source_target_pairs={{0,4},{1,5},{2,6},{3,7},{4,0},{5,1},{6,2},{7,3},{8,12},{9,13},{10,... | collective-permute-start | bytes 1544 | tf_op jit(solution)/shard_map/ppermute | solution.py:251
  108.5 0.1 collective-permute-start.2
  108.7 0.0 copy-done.1
  108.7 0.8 convolution_convert_fusion.2
  109.5 10.3 %fusion.2 = bf16[1,256,3584]{2,1,0:T(8,128)(2,1)} fusion(bf16[2048,256]{1,0:T(8,128)(2,1)S(1)} %bitcast.50, bf16[2048,3584]{1,0:T(8,128)(2,1)} %bitcast.49), kind=kOutput, calls=%fused_computation.4 | convolution fusion | flops 3759013888 | bytes 17563648 | tf_op jit(solution)/shard_map/dot_general | solution.py:257
  119.8 0.0 copy-start
  119.8 0.1 broadcast_multiply_fusion
  120.0 0.0 collective-permute-done.6
  120.0 1.4 %collective-permute-start.1 = (f32[1,128]{1,0:T(1,128)S(1)}, f32[1,128]{1,0:T(1,128)S(1)}, u32[]{:S(2)}, u32[]{:S(2)}) collective-permute-start(f32[1,128]{1,0:T(1,128)S(1)} %get-tuple-element.21), channel_id=1, source_target_pairs={{0,2},{1,3},{2,4},{3,5},{4,6},{5,7},{6,0},{7,1},{8,10},{9,11},{10,... | collective-permute-start | bytes 1544 | tf_op jit(solution)/shard_map/ppermute | solution.py:251
  121.5 0.0 collective-permute-done.5
  121.5 0.7 collective-permute-start
  122.1 0.0 collective-permute-done.4
  122.1 1.2 collective-permute-start.7
  123.4 0.0 collective-permute-done.3
  123.4 0.0 collective-permute-done.2
  123.4 0.4 collective-permute-done.1
  123.8 1.6 %collective-permute-done = f32[1,128]{1,0:T(1,128)S(1)} collective-permute-done((f32[1,128]{1,0:T(1,128)S(1)}, f32[1,128]{1,0:T(1,128)S(1)}, u32[]{:S(2)}, u32[]{:S(2)}) %collective-permute-start) | collective-permute-done | bytes 544 | tf_op jit(solution)/shard_map/ppermute | solution.py:251
  125.3 0.1 select_add_fusion
  125.4 0.0 copy-done
  125.5 0.6 select_reduce_fusion.6
  126.1 5.8 %collective-permute-done.7 = bf16[288,512]{1,0:T(8,128)(2,1)S(1)} collective-permute-done((bf16[288,512]{1,0:T(8,128)(2,1)S(1)}, bf16[288,512]{1,0:T(8,128)(2,1)S(1)}, u32[]{:S(2)}, u32[]{:S(2)}) %collective-permute-start.7) | collective-permute-done | bytes 294944 | tf_op jit(solution)/shard_map/ppermute | solution.py:238
  131.8 0.8 add_convert_fusion
  (18 shorter events, 0.2 us)
Async XLA Ops:
  95.8 12.8 %copy-start.1 = (bf16[4,288,256]{2,1,0:T(8,128)(2,1)S(1)}, bf16[4,288,256]{2,1,0:T(8,128)(2,1)}, u32[]{:S(2)}) copy-start(bf16[4,288,256]{2,1,0:T(8,128)(2,1)} %get-tuple-element.8) | copy-start | bytes 1769476
  103.8 16.2 %collective-permute-start.6 = (f32[1,128]{1,0:T(1,128)S(1)}, f32[1,128]{1,0:T(1,128)S(1)}, u32[]{:S(2)}, u32[]{:S(2)}) collective-permute-start(f32[1,128]{1,0:T(1,128)S(1)} %get-tuple-element.16), channel_id=1, source_target_pairs={{0,7},{1,0},{2,1},{3,2},{4,3},{5,4},{6,5},{7,6},{8,15},{9,8},{10,9... | collective-permute-start | bytes 1544 | tf_op jit(solution)/shard_map/ppermute | solution.py:251
  106.3 15.2 %collective-permute-start.5 = (f32[1,128]{1,0:T(1,128)S(1)}, f32[1,128]{1,0:T(1,128)S(1)}, u32[]{:S(2)}, u32[]{:S(2)}) collective-permute-start(f32[1,128]{1,0:T(1,128)S(1)} %get-tuple-element.17), channel_id=1, source_target_pairs={{0,6},{1,7},{2,0},{3,1},{4,2},{5,3},{6,4},{7,5},{8,14},{9,15},{10,... | collective-permute-start | bytes 1544 | tf_op jit(solution)/shard_map/ppermute | solution.py:251
  106.6 15.5 %collective-permute-start.4 = (f32[1,128]{1,0:T(1,128)S(1)}, f32[1,128]{1,0:T(1,128)S(1)}, u32[]{:S(2)}, u32[]{:S(2)}) collective-permute-start(f32[1,128]{1,0:T(1,128)S(1)} %get-tuple-element.18), channel_id=1, source_target_pairs={{0,5},{1,6},{2,7},{3,0},{4,1},{5,2},{6,3},{7,4},{8,13},{9,14},{10,... | collective-permute-start | bytes 1544 | tf_op jit(solution)/shard_map/ppermute | solution.py:251
  107.1 16.3 %collective-permute-start.3 = (f32[1,128]{1,0:T(1,128)S(1)}, f32[1,128]{1,0:T(1,128)S(1)}, u32[]{:S(2)}, u32[]{:S(2)}) collective-permute-start(f32[1,128]{1,0:T(1,128)S(1)} %get-tuple-element.19), channel_id=1, source_target_pairs={{0,4},{1,5},{2,6},{3,7},{4,0},{5,1},{6,2},{7,3},{8,12},{9,13},{10,... | collective-permute-start | bytes 1544 | tf_op jit(solution)/shard_map/ppermute | solution.py:251
  108.5 14.8 %collective-permute-start.2 = (f32[1,128]{1,0:T(1,128)S(1)}, f32[1,128]{1,0:T(1,128)S(1)}, u32[]{:S(2)}, u32[]{:S(2)}) collective-permute-start(f32[1,128]{1,0:T(1,128)S(1)} %get-tuple-element.20), channel_id=1, source_target_pairs={{0,3},{1,4},{2,5},{3,6},{4,7},{5,0},{6,1},{7,2},{8,11},{9,12},{10,... | collective-permute-start | bytes 1544 | tf_op jit(solution)/shard_map/ppermute | solution.py:251
  119.8 5.6 %copy-start = (s32[128,2]{0,1:T(2,128)S(1)}, s32[128,2]{0,1:T(2,128)}, u32[]{:S(2)}) copy-start(s32[128,2]{0,1:T(2,128)} %param.8) | copy-start | bytes 3076
  120.0 3.7 %collective-permute-start.1 = (f32[1,128]{1,0:T(1,128)S(1)}, f32[1,128]{1,0:T(1,128)S(1)}, u32[]{:S(2)}, u32[]{:S(2)}) collective-permute-start(f32[1,128]{1,0:T(1,128)S(1)} %get-tuple-element.21), channel_id=1, source_target_pairs={{0,2},{1,3},{2,4},{3,5},{4,6},{5,7},{6,0},{7,1},{8,10},{9,11},{10,... | collective-permute-start | bytes 1544 | tf_op jit(solution)/shard_map/ppermute | solution.py:251
  121.5 3.9 %collective-permute-start = (f32[1,128]{1,0:T(1,128)S(1)}, f32[1,128]{1,0:T(1,128)S(1)}, u32[]{:S(2)}, u32[]{:S(2)}) collective-permute-start(f32[1,128]{1,0:T(1,128)S(1)} %get-tuple-element.22), channel_id=1, source_target_pairs={{0,1},{1,2},{2,3},{3,4},{4,5},{5,6},{6,7},{7,0},{8,9},{9,10},{10,1... | collective-permute-start | bytes 1544 | tf_op jit(solution)/shard_map/ppermute | solution.py:251
  122.1 9.7 %collective-permute-start.7 = (bf16[288,512]{1,0:T(8,128)(2,1)S(1)}, bf16[288,512]{1,0:T(8,128)(2,1)S(1)}, u32[]{:S(2)}, u32[]{:S(2)}) collective-permute-start(bf16[288,512]{1,0:T(8,128)(2,1)S(1)} %dynamic-slice_convert_fusion), channel_id=1, source_target_pairs={{0,1},{1,0},{2,3},{3,2},{4,5},{5,4},{6,7},{7,6},{8,9},{9,8},{10,11... | collective-permute-start | bytes 884744 | tf_op jit(solution)/shard_map/ppermute | solution.py:238

commit v3 on v2

--- a/solution.py
+++ b/solution.py
@@ -11,6 +11,7 @@
 gather_limit = 20 * 1024 * 1024
 chunk_rows = 32
 pass_lag = 3
+term_tile_hids = 256
 
 
 def peer(**where):
@@ -24,7 +25,7 @@
     pl.semaphore_wait(barrier, len(peers))
 
 
-def world_kernel(groups, nodes, own_ref, act_ref, facts_ref, out_ref, act_out, facts_out, stage, local_sems,
+def world_kernel(groups, nodes, own_ref, act_ref, facts_ref, w_ref, out_ref, act_out, facts_out, term_ref, stage, w_stage, local_sems,
                  z_recv, right_send, left_send, x_send, x_recv, c_send, c_recv, a_send, a_recv, f_send, f_recv):
     mine, node = lax.axis_index("dp"), lax.axis_index("node")
     chips = nodes // 2
@@ -113,7 +114,21 @@
                     to_chip(source, step, k, distance == 0).wait_recv()
                     to_core(source, step, k, distance == 0).start()
 
-    fetch = pltpu.make_async_copy(own_ref, stage, local_sems.at[0])
+    tokens = own_ref.shape[0]
+
+    def staged(origin):
+        return stage.at[pl.ds(pl.multiple_of(origin * tokens, tokens), tokens)]
+
+    def near_copy(step):
+        origin = lax.rem(node + step, nodes)
+        return pltpu.make_async_copy(out_ref.at[mine, origin], staged(origin), local_sems.at[3 + step])
+
+    def term_tile(tile):
+        hids = pl.ds(tile * term_tile_hids, term_tile_hids)
+        term_ref[:, hids] = lax.dot_general(
+            stage[...], w_stage[hids, :], (((1,), (1,)), ((), ())), preferred_element_type=jnp.float32)
+
+    fetch = pltpu.make_async_copy(own_ref, staged(node), local_sems.at[0])
     fetch.start()
     own_columns = pl.ds(pl.multiple_of(mine * part, part), part)
     keep_act = pltpu.make_async_copy(act_ref.at[:, own_columns], act_out.at[mine], local_sems.at[1])
@@ -127,8 +142,10 @@
     for step in range(1, world):
         fact_copy(step).start()
     fetch.wait()
-    keep = pltpu.make_async_copy(stage, out_ref.at[mine, node], local_sems.at[0])
+    keep = pltpu.make_async_copy(staged(node), out_ref.at[mine, node], local_sems.at[0])
     keep.start()
+    w_copy = pltpu.make_async_copy(w_ref, w_stage, local_sems.at[3])
+    w_copy.start()
 
     order = [(distance, k) for distance in range(groups) for k in range(chunks)]
     for at in range(chunks, len(order) + pass_lag):
@@ -138,6 +155,20 @@
             for item in order[:chunks - pass_lag]:
                 pass_on(*item)
         pass_on(*order[at - pass_lag])
+        if at == 2 * chunks:
+            for k in range(chunks):
+                for step in range(chips):
+                    to_core(mine, step, k, True).wait_recv()
+            for step in range(1, nodes):
+                near_copy(step).start()
+        if at == 2 * chunks + 1:
+            for step in range(1, nodes):
+                near_copy(step).wait()
+            w_copy.wait()
+        if at > 2 * chunks:
+            tile = at - 2 * chunks - 1
+            if tile < term_ref.shape[1] // term_tile_hids:
+                term_tile(tile)
 
     for distance, k in order:
         for side, source, here, further in sides(distance):
@@ -151,7 +182,9 @@
                 for step in range(1, chips):
                     to_chip(source, step, k, distance == 0).wait_send()
                 for step in range(chips):
-                    to_core(source, step, k, distance == 0).wait()
+                    to_core(source, step, k, distance == 0).wait_send()
+                    if distance > 0:
+                        to_core(source, step, k, False).wait_recv()
     for step in range(1, groups):
         act_copy(step).wait()
     for step in range(1, world):
@@ -165,7 +198,7 @@
     return [pl.BlockSpec(memory_space=pl.ANY)] * count
 
 
-def gather_world(d_out, act, facts, groups, nodes):
+def gather_world(d_out, act, facts, weight, groups, nodes):
     chunks, chips = d_out.shape[0] // chunk_rows, nodes // 2
     dma = pltpu.SemaphoreType.DMA
     return pl.pallas_call(
@@ -174,20 +207,22 @@
             jax.ShapeDtypeStruct((groups, nodes) + d_out.shape, d_out.dtype),
             jax.ShapeDtypeStruct((groups, act.shape[0], act.shape[1] // groups), act.dtype),
             jax.ShapeDtypeStruct((groups, nodes) + facts.shape, facts.dtype),
+            jax.ShapeDtypeStruct((nodes * d_out.shape[0], weight.shape[0]), jnp.float32),
         ),
-        in_specs=anywhere(3),
-        out_specs=tuple(anywhere(3)),
+        in_specs=anywhere(4),
+        out_specs=tuple(anywhere(3)) + (pl.BlockSpec(memory_space=pltpu.VMEM),),
         scratch_shapes=[
-            pltpu.VMEM(d_out.shape, d_out.dtype),
-            dma((3,)), dma((groups, chunks)), dma((groups, chunks)), dma((groups, chunks)),
+            pltpu.VMEM((nodes * d_out.shape[0], d_out.shape[1]), d_out.dtype),
+            pltpu.VMEM(weight.shape, weight.dtype),
+            dma((3 + nodes,)), dma((groups, chunks)), dma((groups, chunks)), dma((groups, chunks)),
             dma((groups, chips - 1, chunks)), dma((groups, chips - 1, chunks)),
             dma((groups, chips, chunks)), dma((groups, chips, chunks)),
             dma((groups - 1,)), dma((groups - 1,)),
             dma((groups * nodes - 1,)), dma((groups * nodes - 1,)),
         ],
         cost_estimate=pl.CostEstimate(flops=0, bytes_accessed=200 << 20, transcendentals=0),
-        compiler_params=pltpu.CompilerParams(collective_id=0, has_side_effects=True),
-    )(d_out, act, facts)
+        compiler_params=pltpu.CompilerParams(collective_id=0, has_side_effects=True, vmem_limit_bytes=40 << 20),
+    )(d_out, act, facts, weight)
 
 
 def routing(logits, groups):
@@ -212,9 +247,7 @@
     gates = (route_scale * chosen / totals).astype(jnp.bfloat16).astype(jnp.float32)
     pairs = jnp.concatenate([groups.astype(jnp.float32), slots.astype(jnp.float32), gates], axis=1).T
     pairs = jnp.concatenate([pairs, jnp.zeros((2, tokens), jnp.float32)], axis=0)
-    world, acts, facts = gather_world(d_out, act_rows, pairs, dp_count, node_count)
-    world = world.reshape(dp_count, group_tokens, feat_local)
-    near = lax.dynamic_index_in_dim(world, me_dp, 0, keepdims=False)
+    world, acts, facts, term = gather_world(d_out, act_rows, pairs, weight, dp_count, node_count)
     expert = me_node.astype(jnp.float32)
     live = (facts[:, :, 0:2] == expert) & (facts[:, :, 2:4] >= 0)
     source = jnp.arange(node_count, dtype=jnp.float32)[None, :, None, None] * cap_rows
@@ -225,31 +258,28 @@
     own_where = lax.dynamic_index_in_dim(where, me_dp, 0, keepdims=False)
     own_gate = lax.dynamic_index_in_dim(gate, me_dp, 0, keepdims=False)
     fills = jnp.arange(slot_count, dtype=jnp.int32)[:, None] == own_where[None, :]
-    rows = jnp.dot(
-        fills.astype(jnp.bfloat16), near, preferred_element_type=jnp.float32
-    ).astype(jnp.bfloat16)
-    row_gate = jnp.sum(jnp.where(fills, own_gate[None, :], 0.0), axis=1)
-    term = lax.dot_general(rows, weight, (((1,), (1,)), ((), ())), preferred_element_type=jnp.float32)
-    dot_part = jnp.sum(act_rows.astype(jnp.float32) * term, axis=1)
+    fills = fills.astype(jnp.bfloat16)
+    token_act = lax.dot_general(fills, act_rows, (((0,), (0,)), ((), ())), preferred_element_type=jnp.float32)
+    token_dot = jnp.sum(token_act * term, axis=1)
     half = hid_units // 2
-    gated = row_gate[:, None] * term
-    away = lax.dynamic_slice_in_dim(gated, (1 - me_local) * half, half, axis=1).astype(jnp.bfloat16)
+    gated = (own_gate[:, None] * term).astype(jnp.bfloat16)
+    gated = jnp.dot(fills, gated, preferred_element_type=jnp.float32).astype(jnp.bfloat16)
+    away = lax.dynamic_slice_in_dim(gated, (1 - me_local) * half, half, axis=1)
     home = lax.dynamic_slice_in_dim(gated, me_local * half, half, axis=1)
+    away, token_dot, acts = lax.optimization_barrier((away, token_dot, acts))
     come = lax.ppermute(away, "local", [(0, 1), (1, 0)])
-    d_hidden = (home + come.astype(jnp.float32)).astype(jnp.bfloat16)
+    d_hidden = (home.astype(jnp.float32) + come.astype(jnp.float32)).astype(jnp.bfloat16)
     d_hidden = d_hidden.reshape(1, 1, node_count, cap_rows, half)
 
-    token_dot = jnp.sum(jnp.where(fills, dot_part[:, None], 0.0), axis=0)
     parts = token_dot.reshape(node_count, tokens)
     kept = lax.dynamic_slice_in_dim(parts, me_node, 1, axis=0)
     my_dots = jnp.where(jnp.arange(node_count)[:, None] == me_node, kept, 0.0)
-    members = node_count * 2
-    me = me_node * 2 + me_local
-    for step in range(1, members):
-        target, origin = lax.rem(me + step, members), lax.rem(me - step + members, members)
-        sent = lax.dynamic_slice_in_dim(parts, target // 2, 1, axis=0)
-        got = lax.ppermute(sent, ("node", "local"), [(i, (i + step) % members) for i in range(members)])
-        my_dots = my_dots + jnp.where(jnp.arange(node_count)[:, None] == origin // 2, got, 0.0)
+    for step in range(1, node_count):
+        target, origin = lax.rem(me_node + step, node_count), lax.rem(me_node - step + node_count, node_count)
+        sent = lax.dynamic_slice_in_dim(parts, target, 1, axis=0)
+        got = lax.ppermute(sent, "node", [(i, (i + step) % node_count) for i in range(node_count)])
+        my_dots = my_dots + jnp.where(jnp.arange(node_count)[:, None] == origin, got, 0.0)
+    my_dots = my_dots + lax.ppermute(my_dots, "local", [(0, 1), (1, 0)])
 
     spots = (where[:, :, None] == jnp.arange(slot_count, dtype=jnp.int32)).astype(jnp.bfloat16)
     spots = spots * gate.astype(jnp.bfloat16)[:, :, None]

time: 133 us -> 120 us (0.902)
  waiting for transfers between devices: 7.74 us -> 0.63 us
  matrix products: 18.9 us -> 12.5 us
  local copies, waits for them, and re-layouts: 0.7 us -> 5.41 us
  starting transfers between devices: 8.11 us -> 5.09 us
    dot_general x1 -> x2, matrix products: 7.74 us -> 1.39 us  [the longest x1 0.85 us: gather_shards(): lax.dot_general(fills, act_rows, (((0,), (0,)), ((), ())), preferred_elem...]
    ppermute x1, waiting for transfers between devices: 5.76 us -> 0.01 us  [gather_shards(): come = lax.ppermute(away, 'local', [(0, 1), (1, 0)])]
    unnamed x7 -> x13, local copies, waits for them, and re-layouts: 0.02 us -> 5.34 us
    ppermute x7 -> x4, starting transfers between devices: 6.88 us -> 3.57 us  [the longest x3 2.05 us: gather_shards(): lax.ppermute(sent, 'node', [(i, (i + step) % node_count) for i in range(n...]
    ppermute x7 -> x4, waiting for transfers between devices: 1.98 us -> 0.62 us  [the longest x3 0.62 us: gather_shards(): lax.ppermute(sent, 'node', [(i, (i + step) % node_count) for i in range(n...]
  transfers between devices with their start and end apart: 8 -> 5, of which waited for: 3 -> 1; matrix products, arithmetic and copies ran while one was open for 9% -> 10% of each run, Pallas kernels for 0% -> 0%
where the time goes in v3:
time: 120 us; the launch traced here: 119 us
  Pallas kernels  90.5 us (75%)
  matrix products  12.5 us (10%)
  local copies, waits for them, and re-layouts  5.41 us (5%)
  starting transfers between devices  5.09 us (4%)
  other arithmetic  4.51 us (4%)
    pallas_call x1, Pallas kernels, gather_world(): pl.pallas_call(functools.partial(world_kernel, groups, nodes), out_shape=...  90.5 us
    dot_general x1, matrix products, gather_shards(): lax.dot_general(left.reshape(dp_count * group_tokens, -1), world.reshape(...  10.3 us
    unnamed x13, local copies, waits for them, and re-layouts  5.34 us
  transfers between devices with their start and end apart: 5, of which 1 were waited for; matrix products, arithmetic and copies ran while one was open for 10% of the time, Pallas kernels for 0%

profile of v3, /device:TPU:0, one launch (start us, length us, event | category | flops | bytes accessed | tf_op | source)
XLA Modules:
  0.0 119.5 jit_solution(18061334249812696312)
XLA Ops:
  0.7 0.7 convert_element_type.57
  1.4 0.7 convert_element_type.56
  2.0 0.7 add_divide_fusion
  2.7 0.7 select_reduce_fusion.2
  3.5 0.0 copy-start
  3.5 3.1 %copy-done = bf16[1,1024,3584]{2,1,0:T(8,128)(2,1)S(1)} copy-done((bf16[1,1024,3584]{2,1,0:T(8,128)(2,1)S(1)}, bf16[1,1024,3584]{2,1,0:T(8,128)(2,1)}, u32[]{:S(2)}) %copy-start) | copy-done | bytes 7340056
  6.6 0.0 copy-start.1
  6.6 1.1 copy-done.1
  7.6 0.0 copy-start.3
  7.6 1.2 copy-done.3
  8.8 0.0 copy-start.2
  8.8 90.5 %shard_map.85 = (bf16[4,4,128,3584]{3,2,1,0:T(8,128)(2,1)}, bf16[4,288,256]{2,1,0:T(8,128)(2,1)S(1)}, f32[4,4,8,128]{3,2,1,0:T(8,128)S(1)}, f32[512,1024]{1,0:T(8,128)S(1)}) custom-call(bf16[128,3584]{1,0:T(8,128)(2,1)S(1)} %copy-done.3, bf16[288,1024]{1,0:T(8,128)(2,1)S(1)} %bitcast.36, f32[8,128]{1,0:T(8,128)S(1)} %concatenate.7.facts_ref, ...), custom_call_target="tpu_custom_call" | custom-call | bytes 209715200 | tf_op jit(solution)/shard_map/pallas_call | solution.py:204
  99.3 0.1 select_reduce_fusion.1
  99.5 0.0 copy-done.2
  99.5 0.8 multiply_reduce_fusion
  100.4 0.5 convolution_convert_fusion.2
  101.0 1.5 %collective-permute-start.2 = (f32[1,128]{1,0:T(1,128)S(1)}, f32[1,128]{1,0:T(1,128)S(1)}, u32[]{:S(2)}, u32[]{:S(2)}) collective-permute-start(f32[1,128]{1,0:T(1,128)S(1)} %get-tuple-element.22), channel_id=1, source_target_pairs={{0,6},{2,0},{4,2},{6,4},{1,7},{3,1},{5,3},{7,5},{8,14},{10,8},{12,... | collective-permute-start | bytes 1544 | tf_op jit(solution)/shard_map/ppermute | solution.py:280
  102.5 0.6 collective-permute-start.1
  103.0 0.0 collective-permute-start
  103.0 1.5 %collective-permute-start.4 = (bf16[288,512]{1,0:T(8,128)(2,1)S(1)}, bf16[288,512]{1,0:T(8,128)(2,1)S(1)}, u32[]{:S(2)}, u32[]{:S(2)}) collective-permute-start(bf16[288,512]{1,0:T(8,128)(2,1)S(1)} %constant_dynamic-slice_fusion.4), channel_id=1, source_target_pairs={{0,1},{1,0},{2,3},{3,2},{4,5},{5,4},{6,7},{7,6},{8,9},{9,8},{10,11... | collective-permute-start | bytes 884744 | tf_op jit(solution)/shard_map/ppermute | solution.py:270
  104.6 0.8 convolution_convert_fusion.1
  105.4 0.0 collective-permute-done.2
  105.4 0.6 collective-permute-done.1
  106.0 0.0 collective-permute-done
  106.0 0.1 select_add_fusion
  106.1 1.5 %collective-permute-start.3 = (f32[4,128]{1,0:T(4,128)S(1)}, f32[4,128]{1,0:T(4,128)S(1)}, u32[]{:S(2)}, u32[]{:S(2)}) collective-permute-start(f32[4,128]{1,0:T(4,128)S(1)} %select_add_fusion), channel_id=1, source_target_pairs={{0,1},{1,0},{2,3},{3,2},{4,5},{5,4},{6,7},{7,6},{8,9},{9,8},{10,11... | collective-permute-start | bytes 6152 | tf_op jit(solution)/shard_map/ppermute | solution.py:282
  107.6 0.0 copy-start.4
  107.6 10.3 %fusion = bf16[1,256,3584]{2,1,0:T(8,128)(2,1)} fusion(bf16[2048,256]{1,0:T(8,128)(2,1)S(1)} %bitcast.39, bf16[2048,3584]{1,0:T(8,128)(2,1)} %bitcast.38), kind=kOutput, calls=%fused_computation.1 | convolution fusion | flops 3759013888 | bytes 17563648 | tf_op jit(solution)/shard_map/dot_general | solution.py:287
  117.9 0.0 collective-permute-done.3
  117.9 0.1 add_bitcast_fusion
  118.0 0.0 copy-done.4
  118.1 0.6 select_reduce_fusion.4
  118.7 0.0 collective-permute-done.4
  118.7 0.8 add_convert_fusion
  (17 shorter events, 0.2 us)
Async XLA Ops:
  3.5 3.1 %copy-start = (bf16[1,1024,3584]{2,1,0:T(8,128)(2,1)S(1)}, bf16[1,1024,3584]{2,1,0:T(8,128)(2,1)}, u32[]{:S(2)}) copy-start(bf16[1,1024,3584]{2,1,0:T(8,128)(2,1)} %param.11) | copy-start | bytes 22020100
  6.6 1.1 copy-start.1
  7.6 1.2 copy-start.3
  8.8 90.7 %copy-start.2 = (bf16[1,1,4,72,1024]{4,3,2,1,0:T(8,128)(2,1)S(1)}, bf16[1,1,4,72,1024]{4,3,2,1,0:T(8,128)(2,1)}, u32[]{:S(2)}) copy-start(bf16[1,1,4,72,1024]{4,3,2,1,0:T(8,128)(2,1)} %param.10) | copy-start | bytes 1769476
  101.0 4.4 %collective-permute-start.2 = (f32[1,128]{1,0:T(1,128)S(1)}, f32[1,128]{1,0:T(1,128)S(1)}, u32[]{:S(2)}, u32[]{:S(2)}) collective-permute-start(f32[1,128]{1,0:T(1,128)S(1)} %get-tuple-element.22), channel_id=1, source_target_pairs={{0,6},{2,0},{4,2},{6,4},{1,7},{3,1},{5,3},{7,5},{8,14},{10,8},{12,... | collective-permute-start | bytes 1544 | tf_op jit(solution)/shard_map/ppermute | solution.py:280
  102.5 3.5 %collective-permute-start.1 = (f32[1,128]{1,0:T(1,128)S(1)}, f32[1,128]{1,0:T(1,128)S(1)}, u32[]{:S(2)}, u32[]{:S(2)}) collective-permute-start(f32[1,128]{1,0:T(1,128)S(1)} %get-tuple-element.23), channel_id=1, source_target_pairs={{0,4},{2,6},{4,0},{6,2},{1,5},{3,7},{5,1},{7,3},{8,12},{10,14},{12... | collective-permute-start | bytes 1544 | tf_op jit(solution)/shard_map/ppermute | solution.py:280
  103.0 3.0 %collective-permute-start = (f32[1,128]{1,0:T(1,128)S(1)}, f32[1,128]{1,0:T(1,128)S(1)}, u32[]{:S(2)}, u32[]{:S(2)}) collective-permute-start(f32[1,128]{1,0:T(1,128)S(1)} %get-tuple-element.24), channel_id=1, source_target_pairs={{0,2},{2,4},{4,6},{6,0},{1,3},{3,5},{5,7},{7,1},{8,10},{10,12},{12... | collective-permute-start | bytes 1544 | tf_op jit(solution)/shard_map/ppermute | solution.py:280
  103.0 15.6 %collective-permute-start.4 = (bf16[288,512]{1,0:T(8,128)(2,1)S(1)}, bf16[288,512]{1,0:T(8,128)(2,1)S(1)}, u32[]{:S(2)}, u32[]{:S(2)}) collective-permute-start(bf16[288,512]{1,0:T(8,128)(2,1)S(1)} %constant_dynamic-slice_fusion.4), channel_id=1, source_target_pairs={{0,1},{1,0},{2,3},{3,2},{4,5},{5,4},{6,7},{7,6},{8,9},{9,8},{10,11... | collective-permute-start | bytes 884744 | tf_op jit(solution)/shard_map/ppermute | solution.py:270
  106.1 11.8 %collective-permute-start.3 = (f32[4,128]{1,0:T(4,128)S(1)}, f32[4,128]{1,0:T(4,128)S(1)}, u32[]{:S(2)}, u32[]{:S(2)}) collective-permute-start(f32[4,128]{1,0:T(4,128)S(1)} %select_add_fusion), channel_id=1, source_target_pairs={{0,1},{1,0},{2,3},{3,2},{4,5},{5,4},{6,7},{7,6},{8,9},{9,8},{10,11... | collective-permute-start | bytes 6152 | tf_op jit(solution)/shard_map/ppermute | solution.py:282
  107.6 10.4 %copy-start.4 = (s32[128,2]{0,1:T(2,128)S(1)}, s32[128,2]{0,1:T(2,128)}, u32[]{:S(2)}) copy-start(s32[128,2]{0,1:T(2,128)} %param.8) | copy-start | bytes 3076

commit v4 on v3

--- a/solution.py
+++ b/solution.py
@@ -26,7 +26,7 @@
 
 
 def world_kernel(groups, nodes, own_ref, act_ref, facts_ref, w_ref, out_ref, act_out, facts_out, term_ref, stage, w_stage, local_sems,
-                 z_recv, right_send, left_send, x_send, x_recv, c_send, c_recv, a_send, a_recv, f_send, f_recv):
+                 z_recv, right_send, left_send, x_send, x_recv, c_send, c_recv, a_send, a_recv, f_send, f_recv, cross_send):
     mine, node = lax.axis_index("dp"), lax.axis_index("node")
     chips = nodes // 2
     chip, core = node // 2, node % 2
@@ -64,6 +64,16 @@
             own(k) if first and step == 0 else block(source, origin, k), block(source, origin, k),
             c_send.at[source, step, k], c_recv.at[source, step, k], **peer(node=sibling))
 
+    def crossed(distance, k):
+        return distance == 1 and k == chunks - 1
+
+    def cross(side, step):
+        origin = lax.rem(chip - step + chips, chips) * 2 + core
+        held = block(mine, origin, chunks - 1)
+        return pltpu.make_async_remote_copy(
+            held, held, cross_send.at[(1 - side) // 2, step - 1], x_recv.at[mine, step - 1, chunks - 1],
+            **peer(dp=mine + side))
+
     def act_copy(step):
         target = lax.rem(mine + step, groups)
         columns = pl.ds(pl.multiple_of(target * part, part), part)
@@ -102,8 +112,9 @@
 
             @pl.when(here)
             def _():
-                for step in range(1, chips):
-                    to_chip(source, step, k, False).start()
+                if not crossed(distance, k):
+                    for step in range(1, chips):
+                        to_chip(source, step, k, False).start()
                 to_core(source, 0, k, False).start()
 
     def pass_on(distance, k):
@@ -113,6 +124,12 @@
                 for step in range(1, chips):
                     to_chip(source, step, k, distance == 0).wait_recv()
                     to_core(source, step, k, distance == 0).start()
+        if distance == 0 and k == chunks - 1:
+            for side, source, here, further in sides(0):
+                @pl.when(further)
+                def _():
+                    for step in range(1, chips):
+                        cross(side, step).start()
 
     tokens = own_ref.shape[0]
 
@@ -179,12 +196,18 @@
         for side, source, here, further in sides(distance)[:1 if distance == 0 else 2]:
             @pl.when(here)
             def _():
-                for step in range(1, chips):
-                    to_chip(source, step, k, distance == 0).wait_send()
+                if not crossed(distance, k):
+                    for step in range(1, chips):
+                        to_chip(source, step, k, distance == 0).wait_send()
                 for step in range(chips):
                     to_core(source, step, k, distance == 0).wait_send()
                     if distance > 0:
                         to_core(source, step, k, False).wait_recv()
+    for side, source, here, further in sides(0):
+        @pl.when(further)
+        def _():
+            for step in range(1, chips):
+                cross(side, step).wait_send()
     for step in range(1, groups):
         act_copy(step).wait()
     for step in range(1, world):
@@ -218,10 +241,10 @@
             dma((groups, chips - 1, chunks)), dma((groups, chips - 1, chunks)),
             dma((groups, chips, chunks)), dma((groups, chips, chunks)),
             dma((groups - 1,)), dma((groups - 1,)),
-            dma((groups * nodes - 1,)), dma((groups * nodes - 1,)),
+            dma((groups * nodes - 1,)), dma((groups * nodes - 1,)), dma((2, chips - 1)),
         ],
         cost_estimate=pl.CostEstimate(flops=0, bytes_accessed=200 << 20, transcendentals=0),
-        compiler_params=pltpu.CompilerParams(collective_id=0, has_side_effects=True, vmem_limit_bytes=40 << 20),
+        compiler_params=pltpu.CompilerParams(collective_id=0, has_side_effects=True, vmem_limit_bytes=60 << 20),
     )(d_out, act, facts, weight)
 
 

time: 120 us -> 120 us (level)
  local copies, waits for them, and re-layouts: 5.41 us -> 0.69 us
  Pallas kernels: 90.5 us -> 93.2 us
  matrix products: 12.5 us -> 14.1 us
    unnamed x13 -> x11, local copies, waits for them, and re-layouts: 5.34 us -> 0.03 us
    pallas_call x1, Pallas kernels: 90.5 us -> 93.2 us  [gather_world(): pl.pallas_call(functools.partial(world_kernel, groups, nodes), out_shape=...]
    dot_general x1, matrix products: 0.85 us -> 2.44 us  [gather_shards(): lax.dot_general(fills, act_rows, (((0,), (0,)), ((), ())), preferred_elem...]
where the time goes in v4:
time: 120 us
  Pallas kernels  93.2 us (78%)
  matrix products  14.1 us (12%)
  other arithmetic  5.56 us (5%)
  starting transfers between devices  5.1 us (4%)
    pallas_call x1, Pallas kernels, gather_world(): pl.pallas_call(functools.partial(world_kernel, groups, nodes), out_shape=...  93.2 us
    dot_general x1, matrix products, gather_shards(): lax.dot_general(left.reshape(dp_count * group_tokens, -1), world.reshape(...  10.3 us
    dot_general x1, matrix products, gather_shards(): lax.dot_general(fills, act_rows, (((0,), (0,)), ((), ())), preferred_elem...  2.44 us
  transfers between devices with their start and end apart: 5, of which 1 were waited for; matrix products, arithmetic and copies ran while one was open for 10% of the time, Pallas kernels for 0%

profile of v4, /device:TPU:0, one launch (start us, length us, event | category | flops | bytes accessed | tf_op | source)
XLA Modules:
  0.0 120.1 jit_solution(7399585563871517111)
XLA Ops:
  0.7 0.7 convert_element_type.57
  1.4 0.7 convert_element_type.56
  2.0 0.7 add_divide_fusion
  2.7 0.7 select_reduce_fusion.2
  3.5 0.6 concatenate.7.facts_ref
  4.1 0.0 copy-start.1
  4.1 93.2 %shard_map.85 = (bf16[4,4,128,3584]{3,2,1,0:T(8,128)(2,1)}, bf16[4,288,256]{2,1,0:T(8,128)(2,1)}, f32[4,4,8,128]{3,2,1,0:T(8,128)}, f32[512,1024]{1,0:T(8,128)}) custom-call(bf16[128,3584]{1,0:T(8,128)(2,1)} %own_ref.1, bf16[288,1024]{1,0:T(8,128)(2,1)} %bitcast.37, f32[8,128]{1,0:T(8,128)} %concatenate.7.facts_ref, bf16[1024,3584]{1,0:T(8,128)(2,1)} %bitcast.36), custom_call_target="tpu_custom_call" | custom-call | bytes 209715200 | tf_op jit(solution)/shard_map/pallas_call | solution.py:227
  97.2 0.0 copy-start
  97.3 1.2 select_reduce_fusion.1
  98.5 0.0 copy-done.1
  98.5 2.4 %multiply_reduce_fusion = f32[512]{0:T(512)S(1)} fusion(f32[512,1024]{1,0:T(8,128)} %get-tuple-element.11, bf16[288,1024]{1,0:T(8,128)(2,1)S(1)} %bitcast.38, s32[512]{0:T(512)S(1)} %bitcast.43), kind=kOutput, calls=%fused_computation.4 | convolution fusion | flops 303185408 | bytes 2691072 | tf_op jit(solution)/shard_map/dot_general | solution.py:285
  100.9 0.0 copy-start.3
  100.9 0.0 copy-done
  101.0 0.5 convolution_convert_fusion.2
  101.6 1.5 %collective-permute-start.2 = (f32[1,128]{1,0:T(1,128)S(1)}, f32[1,128]{1,0:T(1,128)S(1)}, u32[]{:S(2)}, u32[]{:S(2)}) collective-permute-start(f32[1,128]{1,0:T(1,128)S(1)} %get-tuple-element.22), channel_id=1, source_target_pairs={{0,6},{2,0},{4,2},{6,4},{1,7},{3,1},{5,3},{7,5},{8,14},{10,8},{12,... | collective-permute-start | bytes 1544 | tf_op jit(solution)/shard_map/ppermute | solution.py:303
  103.1 0.6 collective-permute-start.1
  103.6 0.0 collective-permute-start
  103.6 1.5 %collective-permute-start.4 = (bf16[288,512]{1,0:T(8,128)(2,1)S(1)}, bf16[288,512]{1,0:T(8,128)(2,1)S(1)}, u32[]{:S(2)}, u32[]{:S(2)}) collective-permute-start(bf16[288,512]{1,0:T(8,128)(2,1)S(1)} %constant_dynamic-slice_fusion.4), channel_id=1, source_target_pairs={{0,1},{1,0},{2,3},{3,2},{4,5},{5,4},{6,7},{7,6},{8,9},{9,8},{10,11... | collective-permute-start | bytes 884744 | tf_op jit(solution)/shard_map/ppermute | solution.py:293
  105.2 0.0 copy-done.3
  105.2 0.8 convolution_convert_fusion.1
  106.0 0.0 collective-permute-done.2
  106.0 0.6 collective-permute-done.1
  106.6 0.0 collective-permute-done
  106.6 0.1 select_add_fusion
  106.7 1.5 %collective-permute-start.3 = (f32[4,128]{1,0:T(4,128)S(1)}, f32[4,128]{1,0:T(4,128)S(1)}, u32[]{:S(2)}, u32[]{:S(2)}) collective-permute-start(f32[4,128]{1,0:T(4,128)S(1)} %select_add_fusion), channel_id=1, source_target_pairs={{0,1},{1,0},{2,3},{3,2},{4,5},{5,4},{6,7},{7,6},{8,9},{9,8},{10,11... | collective-permute-start | bytes 6152 | tf_op jit(solution)/shard_map/ppermute | solution.py:305
  108.2 0.0 copy-start.2
  108.2 10.3 %fusion = bf16[1,256,3584]{2,1,0:T(8,128)(2,1)} fusion(bf16[2048,256]{1,0:T(8,128)(2,1)S(1)} %bitcast.39, bf16[2048,3584]{1,0:T(8,128)(2,1)} %bitcast.35), kind=kOutput, calls=%fused_computation.1 | convolution fusion | flops 3759013888 | bytes 17563648 | tf_op jit(solution)/shard_map/dot_general | solution.py:310
  118.5 0.0 collective-permute-done.3
  118.5 0.1 add_bitcast_fusion
  118.6 0.0 copy-done.2
  118.7 0.6 select_reduce_fusion.4
  119.3 0.0 collective-permute-done.4
  119.3 0.8 add_convert_fusion
  (16 shorter events, 0.2 us)
Async XLA Ops:
  4.1 94.4 %copy-start.1 = (bf16[1,1,4,72,1024]{4,3,2,1,0:T(8,128)(2,1)S(1)}, bf16[1,1,4,72,1024]{4,3,2,1,0:T(8,128)(2,1)}, u32[]{:S(2)}) copy-start(bf16[1,1,4,72,1024]{4,3,2,1,0:T(8,128)(2,1)} %param.10) | copy-start | bytes 1769476
  97.2 3.7 %copy-start = (f32[512,1024]{1,0:T(8,128)S(1)}, f32[512,1024]{1,0:T(8,128)}, u32[]{:S(2)}) copy-start(f32[512,1024]{1,0:T(8,128)} %get-tuple-element.11) | copy-start | bytes 6291460
  100.9 4.2 %copy-start.3 = (bf16[4,288,256]{2,1,0:T(8,128)(2,1)S(1)}, bf16[4,288,256]{2,1,0:T(8,128)(2,1)}, u32[]{:S(2)}) copy-start(bf16[4,288,256]{2,1,0:T(8,128)(2,1)} %get-tuple-element.15) | copy-start | bytes 1769476
  101.6 4.4 %collective-permute-start.2 = (f32[1,128]{1,0:T(1,128)S(1)}, f32[1,128]{1,0:T(1,128)S(1)}, u32[]{:S(2)}, u32[]{:S(2)}) collective-permute-start(f32[1,128]{1,0:T(1,128)S(1)} %get-tuple-element.22), channel_id=1, source_target_pairs={{0,6},{2,0},{4,2},{6,4},{1,7},{3,1},{5,3},{7,5},{8,14},{10,8},{12,... | collective-permute-start | bytes 1544 | tf_op jit(solution)/shard_map/ppermute | solution.py:303
  103.1 3.5 %collective-permute-start.1 = (f32[1,128]{1,0:T(1,128)S(1)}, f32[1,128]{1,0:T(1,128)S(1)}, u32[]{:S(2)}, u32[]{:S(2)}) collective-permute-start(f32[1,128]{1,0:T(1,128)S(1)} %get-tuple-element.23), channel_id=1, source_target_pairs={{0,4},{2,6},{4,0},{6,2},{1,5},{3,7},{5,1},{7,3},{8,12},{10,14},{12... | collective-permute-start | bytes 1544 | tf_op jit(solution)/shard_map/ppermute | solution.py:303
  103.6 3.0 %collective-permute-start = (f32[1,128]{1,0:T(1,128)S(1)}, f32[1,128]{1,0:T(1,128)S(1)}, u32[]{:S(2)}, u32[]{:S(2)}) collective-permute-start(f32[1,128]{1,0:T(1,128)S(1)} %get-tuple-element.24), channel_id=1, source_target_pairs={{0,2},{2,4},{4,6},{6,0},{1,3},{3,5},{5,7},{7,1},{8,10},{10,12},{12... | collective-permute-start | bytes 1544 | tf_op jit(solution)/shard_map/ppermute | solution.py:303
  103.6 15.6 %collective-permute-start.4 = (bf16[288,512]{1,0:T(8,128)(2,1)S(1)}, bf16[288,512]{1,0:T(8,128)(2,1)S(1)}, u32[]{:S(2)}, u32[]{:S(2)}) collective-permute-start(bf16[288,512]{1,0:T(8,128)(2,1)S(1)} %constant_dynamic-slice_fusion.4), channel_id=1, source_target_pairs={{0,1},{1,0},{2,3},{3,2},{4,5},{5,4},{6,7},{7,6},{8,9},{9,8},{10,11... | collective-permute-start | bytes 884744 | tf_op jit(solution)/shard_map/ppermute | solution.py:293
  106.7 11.8 %collective-permute-start.3 = (f32[4,128]{1,0:T(4,128)S(1)}, f32[4,128]{1,0:T(4,128)S(1)}, u32[]{:S(2)}, u32[]{:S(2)}) collective-permute-start(f32[4,128]{1,0:T(4,128)S(1)} %select_add_fusion), channel_id=1, source_target_pairs={{0,1},{1,0},{2,3},{3,2},{4,5},{5,4},{6,7},{7,6},{8,9},{9,8},{10,11... | collective-permute-start | bytes 6152 | tf_op jit(solution)/shard_map/ppermute | solution.py:305
  108.2 10.4 %copy-start.2 = (s32[128,2]{0,1:T(2,128)S(1)}, s32[128,2]{0,1:T(2,128)}, u32[]{:S(2)}) copy-start(s32[128,2]{0,1:T(2,128)} %param.8) | copy-start | bytes 3076

commit v5 on v3

--- a/solution.py
+++ b/solution.py
@@ -221,7 +221,7 @@
             dma((groups * nodes - 1,)), dma((groups * nodes - 1,)),
         ],
         cost_estimate=pl.CostEstimate(flops=0, bytes_accessed=200 << 20, transcendentals=0),
-        compiler_params=pltpu.CompilerParams(collective_id=0, has_side_effects=True, vmem_limit_bytes=40 << 20),
+        compiler_params=pltpu.CompilerParams(collective_id=0, has_side_effects=True, vmem_limit_bytes=60 << 20),
     )(d_out, act, facts, weight)
 
 

time: 120 us -> 119 us (level)
  local copies, waits for them, and re-layouts: 5.41 us -> 0.69 us
  matrix products: 12.5 us -> 14.1 us
  Pallas kernels: 90.5 us -> 91.8 us
    unnamed x13 -> x11, local copies, waits for them, and re-layouts: 5.34 us -> 0.03 us
    dot_general x1, matrix products: 0.85 us -> 2.43 us  [gather_shards(): lax.dot_general(fills, act_rows, (((0,), (0,)), ((), ())), preferred_elem...]
    pallas_call x1, Pallas kernels: 90.5 us -> 91.8 us  [gather_world(): pl.pallas_call(functools.partial(world_kernel, groups, nodes), out_shape=...]
where the time goes in v5:
time: 119 us
  Pallas kernels  91.8 us (77%)
  matrix products  14.1 us (12%)
  other arithmetic  5.56 us (5%)
  starting transfers between devices  5.1 us (4%)
    pallas_call x1, Pallas kernels, gather_world(): pl.pallas_call(functools.partial(world_kernel, groups, nodes), out_shape=...  91.8 us
    dot_general x1, matrix products, gather_shards(): lax.dot_general(left.reshape(dp_count * group_tokens, -1), world.reshape(...  10.3 us
    dot_general x1, matrix products, gather_shards(): lax.dot_general(fills, act_rows, (((0,), (0,)), ((), ())), preferred_elem...  2.43 us
  transfers between devices with their start and end apart: 5, of which 1 were waited for; matrix products, arithmetic and copies ran while one was open for 10% of the time, Pallas kernels for 0%

profile of v5, /device:TPU:0, one launch (start us, length us, event | category | flops | bytes accessed | tf_op | source)
XLA Modules:
  0.0 118.7 jit_solution(15346795462400463019)
XLA Ops:
  0.7 0.7 convert_element_type.57
  1.4 0.7 convert_element_type.56
  2.0 0.7 add_divide_fusion
  2.7 0.7 select_reduce_fusion.2
  3.5 0.6 concatenate.7.facts_ref
  4.1 0.0 copy-start.1
  4.1 91.8 %shard_map.85 = (bf16[4,4,128,3584]{3,2,1,0:T(8,128)(2,1)}, bf16[4,288,256]{2,1,0:T(8,128)(2,1)}, f32[4,4,8,128]{3,2,1,0:T(8,128)}, f32[512,1024]{1,0:T(8,128)}) custom-call(bf16[128,3584]{1,0:T(8,128)(2,1)} %own_ref.1, bf16[288,1024]{1,0:T(8,128)(2,1)} %bitcast.37, f32[8,128]{1,0:T(8,128)} %concatenate.7.facts_ref, bf16[1024,3584]{1,0:T(8,128)(2,1)} %bitcast.36), custom_call_target="tpu_custom_call" | custom-call | bytes 209715200 | tf_op jit(solution)/shard_map/pallas_call | solution.py:204
  95.9 0.0 copy-start
  95.9 1.2 select_reduce_fusion.1
  97.1 0.0 copy-done.1
  97.1 2.4 %multiply_reduce_fusion = f32[512]{0:T(512)S(1)} fusion(f32[512,1024]{1,0:T(8,128)} %get-tuple-element.11, bf16[288,1024]{1,0:T(8,128)(2,1)S(1)} %bitcast.38, s32[512]{0:T(512)S(1)} %bitcast.43), kind=kOutput, calls=%fused_computation.4 | convolution fusion | flops 303185408 | bytes 2691072 | tf_op jit(solution)/shard_map/dot_general | solution.py:262
  99.5 0.0 copy-start.3
  99.6 0.0 copy-done
  99.6 0.5 convolution_convert_fusion.2
  100.2 1.5 %collective-permute-start.2 = (f32[1,128]{1,0:T(1,128)S(1)}, f32[1,128]{1,0:T(1,128)S(1)}, u32[]{:S(2)}, u32[]{:S(2)}) collective-permute-start(f32[1,128]{1,0:T(1,128)S(1)} %get-tuple-element.22), channel_id=1, source_target_pairs={{0,6},{2,0},{4,2},{6,4},{1,7},{3,1},{5,3},{7,5},{8,14},{10,8},{12,... | collective-permute-start | bytes 1544 | tf_op jit(solution)/shard_map/ppermute | solution.py:280
  101.7 0.6 collective-permute-start.1
  102.2 0.0 collective-permute-start
  102.2 1.5 %collective-permute-start.4 = (bf16[288,512]{1,0:T(8,128)(2,1)S(1)}, bf16[288,512]{1,0:T(8,128)(2,1)S(1)}, u32[]{:S(2)}, u32[]{:S(2)}) collective-permute-start(bf16[288,512]{1,0:T(8,128)(2,1)S(1)} %constant_dynamic-slice_fusion.4), channel_id=1, source_target_pairs={{0,1},{1,0},{2,3},{3,2},{4,5},{5,4},{6,7},{7,6},{8,9},{9,8},{10,11... | collective-permute-start | bytes 884744 | tf_op jit(solution)/shard_map/ppermute | solution.py:270
  103.8 0.0 copy-done.3
  103.8 0.8 convolution_convert_fusion.1
  104.6 0.0 collective-permute-done.2
  104.6 0.6 collective-permute-done.1
  105.2 0.0 collective-permute-done
  105.2 0.1 select_add_fusion
  105.3 1.5 %collective-permute-start.3 = (f32[4,128]{1,0:T(4,128)S(1)}, f32[4,128]{1,0:T(4,128)S(1)}, u32[]{:S(2)}, u32[]{:S(2)}) collective-permute-start(f32[4,128]{1,0:T(4,128)S(1)} %select_add_fusion), channel_id=1, source_target_pairs={{0,1},{1,0},{2,3},{3,2},{4,5},{5,4},{6,7},{7,6},{8,9},{9,8},{10,11... | collective-permute-start | bytes 6152 | tf_op jit(solution)/shard_map/ppermute | solution.py:282
  106.8 0.0 copy-start.2
  106.8 10.3 %fusion = bf16[1,256,3584]{2,1,0:T(8,128)(2,1)} fusion(bf16[2048,256]{1,0:T(8,128)(2,1)S(1)} %bitcast.39, bf16[2048,3584]{1,0:T(8,128)(2,1)} %bitcast.35), kind=kOutput, calls=%fused_computation.1 | convolution fusion | flops 3759013888 | bytes 17563648 | tf_op jit(solution)/shard_map/dot_general | solution.py:287
  117.2 0.0 collective-permute-done.3
  117.2 0.1 add_bitcast_fusion
  117.2 0.0 copy-done.2
  117.3 0.6 select_reduce_fusion.4
  117.9 0.0 collective-permute-done.4
  117.9 0.8 add_convert_fusion
  (16 shorter events, 0.2 us)
Async XLA Ops:
  4.1 93.1 %copy-start.1 = (bf16[1,1,4,72,1024]{4,3,2,1,0:T(8,128)(2,1)S(1)}, bf16[1,1,4,72,1024]{4,3,2,1,0:T(8,128)(2,1)}, u32[]{:S(2)}) copy-start(bf16[1,1,4,72,1024]{4,3,2,1,0:T(8,128)(2,1)} %param.10) | copy-start | bytes 1769476
  95.9 3.7 %copy-start = (f32[512,1024]{1,0:T(8,128)S(1)}, f32[512,1024]{1,0:T(8,128)}, u32[]{:S(2)}) copy-start(f32[512,1024]{1,0:T(8,128)} %get-tuple-element.11) | copy-start | bytes 6291460
  99.5 4.2 %copy-start.3 = (bf16[4,288,256]{2,1,0:T(8,128)(2,1)S(1)}, bf16[4,288,256]{2,1,0:T(8,128)(2,1)}, u32[]{:S(2)}) copy-start(bf16[4,288,256]{2,1,0:T(8,128)(2,1)} %get-tuple-element.15) | copy-start | bytes 1769476
  100.2 4.4 %collective-permute-start.2 = (f32[1,128]{1,0:T(1,128)S(1)}, f32[1,128]{1,0:T(1,128)S(1)}, u32[]{:S(2)}, u32[]{:S(2)}) collective-permute-start(f32[1,128]{1,0:T(1,128)S(1)} %get-tuple-element.22), channel_id=1, source_target_pairs={{0,6},{2,0},{4,2},{6,4},{1,7},{3,1},{5,3},{7,5},{8,14},{10,8},{12,... | collective-permute-start | bytes 1544 | tf_op jit(solution)/shard_map/ppermute | solution.py:280
  101.7 3.5 %collective-permute-start.1 = (f32[1,128]{1,0:T(1,128)S(1)}, f32[1,128]{1,0:T(1,128)S(1)}, u32[]{:S(2)}, u32[]{:S(2)}) collective-permute-start(f32[1,128]{1,0:T(1,128)S(1)} %get-tuple-element.23), channel_id=1, source_target_pairs={{0,4},{2,6},{4,0},{6,2},{1,5},{3,7},{5,1},{7,3},{8,12},{10,14},{12... | collective-permute-start | bytes 1544 | tf_op jit(solution)/shard_map/ppermute | solution.py:280
  102.2 3.0 %collective-permute-start = (f32[1,128]{1,0:T(1,128)S(1)}, f32[1,128]{1,0:T(1,128)S(1)}, u32[]{:S(2)}, u32[]{:S(2)}) collective-permute-start(f32[1,128]{1,0:T(1,128)S(1)} %get-tuple-element.24), channel_id=1, source_target_pairs={{0,2},{2,4},{4,6},{6,0},{1,3},{3,5},{5,7},{7,1},{8,10},{10,12},{12... | collective-permute-start | bytes 1544 | tf_op jit(solution)/shard_map/ppermute | solution.py:280
  102.2 15.6 %collective-permute-start.4 = (bf16[288,512]{1,0:T(8,128)(2,1)S(1)}, bf16[288,512]{1,0:T(8,128)(2,1)S(1)}, u32[]{:S(2)}, u32[]{:S(2)}) collective-permute-start(bf16[288,512]{1,0:T(8,128)(2,1)S(1)} %constant_dynamic-slice_fusion.4), channel_id=1, source_target_pairs={{0,1},{1,0},{2,3},{3,2},{4,5},{5,4},{6,7},{7,6},{8,9},{9,8},{10,11... | collective-permute-start | bytes 884744 | tf_op jit(solution)/shard_map/ppermute | solution.py:270
  105.3 11.9 %collective-permute-start.3 = (f32[4,128]{1,0:T(4,128)S(1)}, f32[4,128]{1,0:T(4,128)S(1)}, u32[]{:S(2)}, u32[]{:S(2)}) collective-permute-start(f32[4,128]{1,0:T(4,128)S(1)} %select_add_fusion), channel_id=1, source_target_pairs={{0,1},{1,0},{2,3},{3,2},{4,5},{5,4},{6,7},{7,6},{8,9},{9,8},{10,11... | collective-permute-start | bytes 6152 | tf_op jit(solution)/shard_map/ppermute | solution.py:282
  106.8 10.4 %copy-start.2 = (s32[128,2]{0,1:T(2,128)S(1)}, s32[128,2]{0,1:T(2,128)}, u32[]{:S(2)}) copy-start(s32[128,2]{0,1:T(2,128)} %param.8) | copy-start | bytes 3076

commit v6 on v5

--- a/solution.py
+++ b/solution.py
@@ -137,8 +137,6 @@
     keep_facts.start()
     for k in range(chunks):
         spread(0, k)
-    for step in range(1, groups):
-        act_copy(step).start()
     for step in range(1, world):
         fact_copy(step).start()
     fetch.wait()
@@ -156,6 +154,8 @@
                 pass_on(*item)
         pass_on(*order[at - pass_lag])
         if at == 2 * chunks:
+            for step in range(1, groups):
+                act_copy(step).start()
             for k in range(chunks):
                 for step in range(chips):
                     to_core(mine, step, k, True).wait_recv()

time: 119 us -> 119 us (level)
  no operation moved by 1% of the time
where the time goes in v6:
time: 119 us
  Pallas kernels  91.8 us (77%)
  matrix products  14.1 us (12%)
  other arithmetic  5.56 us (5%)
  starting transfers between devices  5.1 us (4%)
    pallas_call x1, Pallas kernels, gather_world(): pl.pallas_call(functools.partial(world_kernel, groups, nodes), out_shape=...  91.8 us
    dot_general x1, matrix products, gather_shards(): lax.dot_general(left.reshape(dp_count * group_tokens, -1), world.reshape(...  10.3 us
    dot_general x1, matrix products, gather_shards(): lax.dot_general(fills, act_rows, (((0,), (0,)), ((), ())), preferred_elem...  2.43 us
  transfers between devices with their start and end apart: 5, of which 1 were waited for; matrix products, arithmetic and copies ran while one was open for 10% of the time, Pallas kernels for 0%

profile of v6, /device:TPU:0, one launch (start us, length us, event | category | flops | bytes accessed | tf_op | source)
XLA Modules:
  0.0 118.7 jit_solution(6384507031519767333)
XLA Ops:
  0.7 0.7 convert_element_type.57
  1.4 0.7 convert_element_type.56
  2.0 0.7 add_divide_fusion
  2.7 0.7 select_reduce_fusion.2
  3.5 0.6 concatenate.7.facts_ref
  4.1 0.0 copy-start.1
  4.1 91.8 %shard_map.85 = (bf16[4,4,128,3584]{3,2,1,0:T(8,128)(2,1)}, bf16[4,288,256]{2,1,0:T(8,128)(2,1)}, f32[4,4,8,128]{3,2,1,0:T(8,128)}, f32[512,1024]{1,0:T(8,128)}) custom-call(bf16[128,3584]{1,0:T(8,128)(2,1)} %own_ref.1, bf16[288,1024]{1,0:T(8,128)(2,1)} %bitcast.37, f32[8,128]{1,0:T(8,128)} %concatenate.7.facts_ref, bf16[1024,3584]{1,0:T(8,128)(2,1)} %bitcast.36), custom_call_target="tpu_custom_call" | custom-call | bytes 209715200 | tf_op jit(solution)/shard_map/pallas_call | solution.py:204
  95.9 0.0 copy-start
  95.9 1.2 select_reduce_fusion.1
  97.1 0.0 copy-done.1
  97.1 2.4 %multiply_reduce_fusion = f32[512]{0:T(512)S(1)} fusion(f32[512,1024]{1,0:T(8,128)} %get-tuple-element.11, bf16[288,1024]{1,0:T(8,128)(2,1)S(1)} %bitcast.38, s32[512]{0:T(512)S(1)} %bitcast.43), kind=kOutput, calls=%fused_computation.4 | convolution fusion | flops 303185408 | bytes 2691072 | tf_op jit(solution)/shard_map/dot_general | solution.py:262
  99.5 0.0 copy-start.3
  99.6 0.0 copy-done
  99.6 0.5 convolution_convert_fusion.2
  100.2 1.5 %collective-permute-start.2 = (f32[1,128]{1,0:T(1,128)S(1)}, f32[1,128]{1,0:T(1,128)S(1)}, u32[]{:S(2)}, u32[]{:S(2)}) collective-permute-start(f32[1,128]{1,0:T(1,128)S(1)} %get-tuple-element.22), channel_id=1, source_target_pairs={{0,6},{2,0},{4,2},{6,4},{1,7},{3,1},{5,3},{7,5},{8,14},{10,8},{12,... | collective-permute-start | bytes 1544 | tf_op jit(solution)/shard_map/ppermute | solution.py:280
  101.7 0.6 collective-permute-start.1
  102.2 0.0 collective-permute-start
  102.2 1.5 %collective-permute-start.4 = (bf16[288,512]{1,0:T(8,128)(2,1)S(1)}, bf16[288,512]{1,0:T(8,128)(2,1)S(1)}, u32[]{:S(2)}, u32[]{:S(2)}) collective-permute-start(bf16[288,512]{1,0:T(8,128)(2,1)S(1)} %constant_dynamic-slice_fusion.4), channel_id=1, source_target_pairs={{0,1},{1,0},{2,3},{3,2},{4,5},{5,4},{6,7},{7,6},{8,9},{9,8},{10,11... | collective-permute-start | bytes 884744 | tf_op jit(solution)/shard_map/ppermute | solution.py:270
  103.8 0.0 copy-done.3
  103.8 0.8 convolution_convert_fusion.1
  104.6 0.0 collective-permute-done.2
  104.6 0.6 collective-permute-done.1
  105.2 0.0 collective-permute-done
  105.2 0.1 select_add_fusion
  105.3 1.5 %collective-permute-start.3 = (f32[4,128]{1,0:T(4,128)S(1)}, f32[4,128]{1,0:T(4,128)S(1)}, u32[]{:S(2)}, u32[]{:S(2)}) collective-permute-start(f32[4,128]{1,0:T(4,128)S(1)} %select_add_fusion), channel_id=1, source_target_pairs={{0,1},{1,0},{2,3},{3,2},{4,5},{5,4},{6,7},{7,6},{8,9},{9,8},{10,11... | collective-permute-start | bytes 6152 | tf_op jit(solution)/shard_map/ppermute | solution.py:282
  106.8 0.0 copy-start.2
  106.8 10.3 %fusion = bf16[1,256,3584]{2,1,0:T(8,128)(2,1)} fusion(bf16[2048,256]{1,0:T(8,128)(2,1)S(1)} %bitcast.39, bf16[2048,3584]{1,0:T(8,128)(2,1)} %bitcast.35), kind=kOutput, calls=%fused_computation.1 | convolution fusion | flops 3759013888 | bytes 17563648 | tf_op jit(solution)/shard_map/dot_general | solution.py:287
  117.2 0.0 collective-permute-done.3
  117.2 0.1 add_bitcast_fusion
  117.2 0.0 copy-done.2
  117.3 0.6 select_reduce_fusion.4
  117.9 0.0 collective-permute-done.4
  117.9 0.8 add_convert_fusion
  (16 shorter events, 0.2 us)
Async XLA Ops:
  4.1 93.1 %copy-start.1 = (bf16[1,1,4,72,1024]{4,3,2,1,0:T(8,128)(2,1)S(1)}, bf16[1,1,4,72,1024]{4,3,2,1,0:T(8,128)(2,1)}, u32[]{:S(2)}) copy-start(bf16[1,1,4,72,1024]{4,3,2,1,0:T(8,128)(2,1)} %param.10) | copy-start | bytes 1769476
  95.9 3.7 %copy-start = (f32[512,1024]{1,0:T(8,128)S(1)}, f32[512,1024]{1,0:T(8,128)}, u32[]{:S(2)}) copy-start(f32[512,1024]{1,0:T(8,128)} %get-tuple-element.11) | copy-start | bytes 6291460
  99.5 4.2 %copy-start.3 = (bf16[4,288,256]{2,1,0:T(8,128)(2,1)S(1)}, bf16[4,288,256]{2,1,0:T(8,128)(2,1)}, u32[]{:S(2)}) copy-start(bf16[4,288,256]{2,1,0:T(8,128)(2,1)} %get-tuple-element.15) | copy-start | bytes 1769476
  100.2 4.4 %collective-permute-start.2 = (f32[1,128]{1,0:T(1,128)S(1)}, f32[1,128]{1,0:T(1,128)S(1)}, u32[]{:S(2)}, u32[]{:S(2)}) collective-permute-start(f32[1,128]{1,0:T(1,128)S(1)} %get-tuple-element.22), channel_id=1, source_target_pairs={{0,6},{2,0},{4,2},{6,4},{1,7},{3,1},{5,3},{7,5},{8,14},{10,8},{12,... | collective-permute-start | bytes 1544 | tf_op jit(solution)/shard_map/ppermute | solution.py:280
  101.7 3.5 %collective-permute-start.1 = (f32[1,128]{1,0:T(1,128)S(1)}, f32[1,128]{1,0:T(1,128)S(1)}, u32[]{:S(2)}, u32[]{:S(2)}) collective-permute-start(f32[1,128]{1,0:T(1,128)S(1)} %get-tuple-element.23), channel_id=1, source_target_pairs={{0,4},{2,6},{4,0},{6,2},{1,5},{3,7},{5,1},{7,3},{8,12},{10,14},{12... | collective-permute-start | bytes 1544 | tf_op jit(solution)/shard_map/ppermute | solution.py:280
  102.2 3.0 %collective-permute-start = (f32[1,128]{1,0:T(1,128)S(1)}, f32[1,128]{1,0:T(1,128)S(1)}, u32[]{:S(2)}, u32[]{:S(2)}) collective-permute-start(f32[1,128]{1,0:T(1,128)S(1)} %get-tuple-element.24), channel_id=1, source_target_pairs={{0,2},{2,4},{4,6},{6,0},{1,3},{3,5},{5,7},{7,1},{8,10},{10,12},{12... | collective-permute-start | bytes 1544 | tf_op jit(solution)/shard_map/ppermute | solution.py:280
  102.2 15.6 %collective-permute-start.4 = (bf16[288,512]{1,0:T(8,128)(2,1)S(1)}, bf16[288,512]{1,0:T(8,128)(2,1)S(1)}, u32[]{:S(2)}, u32[]{:S(2)}) collective-permute-start(bf16[288,512]{1,0:T(8,128)(2,1)S(1)} %constant_dynamic-slice_fusion.4), channel_id=1, source_target_pairs={{0,1},{1,0},{2,3},{3,2},{4,5},{5,4},{6,7},{7,6},{8,9},{9,8},{10,11... | collective-permute-start | bytes 884744 | tf_op jit(solution)/shard_map/ppermute | solution.py:270
  105.3 11.9 %collective-permute-start.3 = (f32[4,128]{1,0:T(4,128)S(1)}, f32[4,128]{1,0:T(4,128)S(1)}, u32[]{:S(2)}, u32[]{:S(2)}) collective-permute-start(f32[4,128]{1,0:T(4,128)S(1)} %select_add_fusion), channel_id=1, source_target_pairs={{0,1},{1,0},{2,3},{3,2},{4,5},{5,4},{6,7},{7,6},{8,9},{9,8},{10,11... | collective-permute-start | bytes 6152 | tf_op jit(solution)/shard_map/ppermute | solution.py:282
  106.8 10.4 %copy-start.2 = (s32[128,2]{0,1:T(2,128)S(1)}, s32[128,2]{0,1:T(2,128)}, u32[]{:S(2)}) copy-start(s32[128,2]{0,1:T(2,128)} %param.8) | copy-start | bytes 3076
